TPU v7x, 256 devices: a whole 4x4x8 slice. The times are simulated.
256 devices in a mesh: gx: 16 (over z, core), gy: 16 (over x, y).
Axes of the slice: x: 4, y: 4, z: 8, core: 2. Of those that a mesh axis runs over, the one named last changes fastest.
Arguments:
- ensemble: float32 [128, 384, 2048], P('gx', 'gy'), may hold values from -6 to 6
- weights: float32 [4, 128, 12288], P(None, 'gx', 'gy'), may hold values from 0.02 to 0.22
- obs_cell: int32 [3, 512], replicated, may hold values from 0 to 383, as said below
- obs_batch: int32 [512], replicated, may hold values from 0 to 3, as said below
- obs_radius: int32 [512], replicated, may hold values from 24 to 48
- obs_value: float32 [512], replicated, may hold values from -8 to 8
- obs_noise: float32 [64, 512], replicated, may hold values from -6 to 6
- obs_var: float32 [512], replicated, may hold values from 0.25 to 1
Outputs:
- analysis: float32 [128, 384, 2048], P('gx', 'gy')
Inputs may be any that keep to these rules, and one draw needn't show every extreme that they name: `obs_cell`: row 0 is an x below 128, row 1 a y below 384, row 2 a level below 32; observations cluster in a few regions. `obs_batch`: each batch number occurs exactly 128 times.
All inputs are finite; a program needn't handle non-finite values.
Results may differ from a plain program's by a relative error of at most 0.0003.
Values sent between devices are 32-bit elements; how exact they have to be, the bound alone decides.
A program may use at most 128 MiB of HBM per device.

v0:
```python
import jax
import jax.numpy as jnp
from jax import lax
from jax.sharding import PartitionSpec as P

MEM = 64
LEV = 32
OBS_B = 128
NBATCH = 4


HIGHEST = lax.Precision.HIGHEST
VERTICAL_SCALE = 8.0


def padded_2(cells, sides, width):
    for axis, dim in sides:
        count = lax.axis_size(axis)
        ends = count - 1
        head = lax.slice_in_dim(cells, 0, width, axis=dim)
        tail = lax.slice_in_dim(cells, cells.shape[dim] - width, cells.shape[dim], axis=dim)
        cells = jnp.concatenate(
            [
                lax.ppermute(tail, axis, [(i, (i + 1) % count) for i in range(ends)]),
                cells,
                lax.ppermute(head, axis, [((i + 1) % count, i) for i in range(ends)]),
            ],
            axis=dim,
        )
    return cells


def horizontal_taper(delta_x, delta_y, radius):
    distance_ratio = (delta_x * delta_x + delta_y * delta_y) / (radius * radius)
    return jnp.square(jnp.maximum(1.0 - distance_ratio, 0.0))


def level_taper(delta_l):
    return 1.0 / (1.0 + jnp.square(delta_l / VERTICAL_SCALE))


def solve_batch(prior_obs, obs_value, obs_noise, variance):
    anomaly = prior_obs - jnp.mean(prior_obs, axis=0, keepdims=True)
    covariance = jnp.dot(anomaly.T, anomaly, precision=HIGHEST) / (MEM - 1) + jnp.diag(variance)
    innovation = obs_value[None, :] + jnp.sqrt(variance)[None, :] * obs_noise - prior_obs
    factor = jnp.linalg.cholesky(covariance)
    solved = jax.scipy.linalg.cho_solve((factor, True), innovation.T)
    return (anomaly, solved.T)


def body(ensemble, weights, obs_cell, obs_batch, obs_radius, obs_value, obs_noise, obs_var):
    rows_x = ensemble.shape[0]
    rows_y = ensemble.shape[1]
    point_count = rows_x * rows_y * LEV
    start_x = lax.axis_index("gx") * rows_x
    start_y = lax.axis_index("gy") * rows_y
    centre = ensemble.reshape(rows_x, rows_y, LEV, MEM)
    coeffs = weights.reshape(4, rows_x, rows_y, LEV, 1)
    padded = padded_2(ensemble, (("gx", 0), ("gy", 1)), 1)
    padded = padded.reshape(rows_x + 2, rows_y + 2, LEV, MEM)
    from_west = padded[:-2, 1:-1]
    from_east = padded[2:, 1:-1]
    from_south = padded[1:-1, :-2]
    from_north = padded[1:-1, 2:]
    stepped = (
        centre
        + coeffs[0] * (from_west - centre)
        + coeffs[1] * (from_east - centre)
        + coeffs[2] * (from_south - centre)
        + coeffs[3] * (from_north - centre)
    )
    analysis = stepped.reshape(point_count, MEM).T
    cells_x = (start_x + jnp.arange(rows_x)).astype(jnp.float32)
    cells_y = (start_y + jnp.arange(rows_y)).astype(jnp.float32)
    levels = jnp.arange(LEV).astype(jnp.float32)
    batch_order = jnp.argsort(obs_batch, stable=True)
    for batch_number in range(NBATCH):
        chosen = batch_order[batch_number * OBS_B : (batch_number + 1) * OBS_B]
        obs_x = obs_cell[0][chosen]
        obs_y = obs_cell[1][chosen]
        obs_l = obs_cell[2][chosen]
        inside = (
            (obs_x >= start_x)
            & (obs_x < start_x + rows_x)
            & (obs_y >= start_y)
            & (obs_y < start_y + rows_y)
        )
        flat_index = ((obs_x - start_x) * rows_y + (obs_y - start_y)) * LEV + obs_l
        flat_index = jnp.clip(flat_index, 0, point_count - 1)
        prior_obs = lax.psum(
            jnp.where(inside[None, :], jnp.take(analysis, flat_index, axis=1), 0.0), ("gx", "gy")
        )
        anomaly, gain_rows = solve_batch(
            prior_obs, obs_value[chosen], obs_noise[:, chosen], obs_var[chosen]
        )
        radius = obs_radius[chosen].astype(jnp.float32)
        fx = obs_x.astype(jnp.float32)
        fy = obs_y.astype(jnp.float32)
        fl = obs_l.astype(jnp.float32)
        across = horizontal_taper(
            cells_x[None, :, None] - fx[:, None, None],
            cells_y[None, None, :] - fy[:, None, None],
            radius[:, None, None],
        )
        vertical = level_taper(levels[None, :] - fl[:, None])
        loc_taper = (across[:, :, :, None] * vertical[:, None, None, :]).reshape(OBS_B, point_count)
        centred = analysis - jnp.mean(analysis, axis=0, keepdims=True)
        link = jnp.dot(anomaly.T, centred, precision=HIGHEST) / (MEM - 1) * loc_taper
        analysis = analysis + jnp.dot(gain_rows, link, precision=HIGHEST)
    return analysis.T.reshape(rows_x, rows_y, LEV * MEM)


def solution(mesh):
    placed = (P("gx", "gy", None), P(None, "gx", "gy"), P(), P(), P(), P(), P(), P())
    return jax.shard_map(
        body, mesh=mesh, in_specs=placed, out_specs=P("gx", "gy", None), check_vma=False
    )
```

profile of v0, /device:TPU:1, one launch (start us, length us, event | category | flops | bytes accessed | tf_op | source)
XLA Modules:
  0.0 575.5 jit_solution(16238578814544445766)
XLA Ops:
  1.9 4.9 collective-permute-start
  11.4 2.6 reshape.608
  13.9 3.8 sort.17
  60.1 3.5 copy.119
  66.3 3.6 copy.125
  72.5 15.9 %copy.130 = f32[128,6144]{1,0:T(8,128)} copy(f32[128,6144]{0,1:T(8,128)} %bitcast.139) | data formatting | bytes 6291456 | tf_op jit(solution)/shard_map/mul | solution.py:106
  91.6 3.6 copy.132
  97.5 3.0 collective-permute-start.2
  102.6 4.1 collective-permute-done.3
  108.6 3.1 reshape.609
  111.6 9.6 %fusion.86 = (f32[8,24,32]{2,1,0:T(8,128)S(1)}, f32[8,24,32,64]{3,2,1,0:T(8,128)S(1)}) fusion(f32[8,24,32,64]{3,2,1,0:T(8,128)} %reshape.608, f32[10,26,32,64]{3,2,1,0:T(8,128)} %reshape.609, f32[8,24,32]{2,1,0:T(8,128)} %mul.287, f32[8,24,32]{2,1,0:T(8,128)} %mul.284, f32[8,24,32]{2,1,0:T(8,128)S(1)} %mul.281, f32[8,24,32]{2,1,0:T(8,128)S(1)} %mul.278), kind=kLoop, calls=%fused_computation.226 | loop fusion | flops 5105664 | bytes 9560064 | tf_op jit(solution)/shard_map/reduce_sum | solution.py:107
  122.0 81.0 %psum.28 = f32[64,128]{0,1:T(8,128)S(1)} all-reduce(f32[64,128]{0,1:T(8,128)S(1)} %bitcast_select_fusion.3), channel_id=1, replica_groups=mesh['gx'=16,'gy'=16] {'gx','gy'}, use_global_device_ids=true, to_apply=%region_1.3 | all-reduce | flops 8192 | bytes 65536 | tf_op jit(solution)/shard_map/psum | solution.py:90
  206.1 11.7 %cholesky.74 = f32[128,128]{1,0:T(8,128)S(1)} custom-call(f32[128,128]{1,0:T(8,128)S(1)} %fusion.50), custom_call_target="Cholesky" | custom-call | tf_op jit(solution)/shard_map/jit(cholesky)/cholesky | solution.py:46
  219.2 9.8 %custom-call.10 = f32[1,128,128]{1,2,0:T(8,128)S(1)} custom-call(f32[1,128,128]{2,1,0:T(8,128)S(1)} %fusion.23), custom_call_target="InvertDiagBlocksLowerTriangular" | custom-call | tf_op jit(solution)/shard_map/jit(_cho_solve)/triangular_solve | solution.py:47
  229.6 4.8 fusion.3
  234.4 3.0 fusion.85
  242.4 74.4 %psum.29 = f32[64,128]{0,1:T(8,128)S(1)} all-reduce(f32[64,128]{0,1:T(8,128)S(1)} %bitcast_select_fusion.2), channel_id=1, replica_groups=mesh['gx'=16,'gy'=16] {'gx','gy'}, use_global_device_ids=true, to_apply=%region_6.10 | all-reduce | flops 8192 | bytes 65536 | tf_op jit(solution)/shard_map/psum | solution.py:90
  317.3 11.7 %cholesky.85 = f32[128,128]{1,0:T(8,128)S(1)} custom-call(f32[128,128]{1,0:T(8,128)S(1)} %fusion.44), custom_call_target="Cholesky" | custom-call | tf_op jit(solution)/shard_map/jit(cholesky)/cholesky | solution.py:46
  330.4 9.8 %custom-call.11 = f32[1,128,128]{1,2,0:T(8,128)S(1)} custom-call(f32[1,128,128]{2,1,0:T(8,128)S(1)} %fusion.24), custom_call_target="InvertDiagBlocksLowerTriangular" | custom-call | tf_op jit(solution)/shard_map/jit(_cho_solve)/triangular_solve | solution.py:47
  340.9 4.8 fusion.2
  345.7 3.2 fusion.84
  351.3 2.5 gather_fusion.30
  353.9 73.5 %psum.30 = f32[64,128]{0,1:T(8,128)S(1)} all-reduce(f32[64,128]{0,1:T(8,128)S(1)} %bitcast_select_fusion.1), channel_id=1, replica_groups=mesh['gx'=16,'gy'=16] {'gx','gy'}, use_global_device_ids=true, to_apply=%region_9.13 | all-reduce | flops 8192 | bytes 65536 | tf_op jit(solution)/shard_map/psum | solution.py:90
  428.0 11.7 %cholesky.96 = f32[128,128]{1,0:T(8,128)S(1)} custom-call(f32[128,128]{1,0:T(8,128)S(1)} %fusion.38), custom_call_target="Cholesky" | custom-call | tf_op jit(solution)/shard_map/jit(cholesky)/cholesky | solution.py:46
  441.1 9.8 %custom-call.12 = f32[1,128,128]{1,2,0:T(8,128)S(1)} custom-call(f32[1,128,128]{2,1,0:T(8,128)S(1)} %fusion.25), custom_call_target="InvertDiagBlocksLowerTriangular" | custom-call | tf_op jit(solution)/shard_map/jit(_cho_solve)/triangular_solve | solution.py:47
  451.6 4.8 fusion.1
  456.3 3.1 fusion.83
  464.5 74.0 %psum.31 = f32[64,128]{0,1:T(8,128)S(1)} all-reduce(f32[64,128]{0,1:T(8,128)S(1)} %bitcast_select_fusion), channel_id=1, replica_groups=mesh['gx'=16,'gy'=16] {'gx','gy'}, use_global_device_ids=true, to_apply=%region_12.16 | all-reduce | flops 8192 | bytes 65536 | tf_op jit(solution)/shard_map/psum | solution.py:90
  539.1 11.7 %cholesky.107 = f32[128,128]{1,0:T(8,128)S(1)} custom-call(f32[128,128]{1,0:T(8,128)S(1)} %fusion.32), custom_call_target="Cholesky" | custom-call | tf_op jit(solution)/shard_map/jit(cholesky)/cholesky | solution.py:46
  552.2 9.8 %custom-call.13 = f32[1,128,128]{1,2,0:T(8,128)S(1)} custom-call(f32[1,128,128]{2,1,0:T(8,128)S(1)} %fusion.26), custom_call_target="InvertDiagBlocksLowerTriangular" | custom-call | tf_op jit(solution)/shard_map/jit(_cho_solve)/triangular_solve | solution.py:47
  562.7 4.9 fusion
  567.6 3.4 convolution_add_fusion
  (221 shorter events, 92.8 us)
Async XLA Ops:
  0.0 35.8 %copy-start = (f32[512]{0:T(512)S(1)}, f32[512]{0:T(512)}, u32[]{:S(2)}) copy-start(f32[512]{0:T(512)} %param.20) | copy-start | bytes 6148
  0.0 11.3 %copy-start.7 = (f32[8,24,2048]{2,1,0:T(8,128)S(1)}, f32[8,24,2048]{2,1,0:T(8,128)}, u32[]{:S(2)}) copy-start(f32[8,24,2048]{2,1,0:T(8,128)} %param.13) | copy-start | bytes 4718596
  1.9 93.3 %collective-permute-start = (f32[1,24,2048]{2,1,0:T(8,128)}, f32[1,24,2048]{2,1,0:T(8,128)}, u32[]{:S(2)}, u32[]{:S(2)}) collective-permute-start(f32[1,24,2048]{2,1,0:T(8,128)} %get-tuple-element.28), channel_id=1, source_target_pairs={{0,16},{16,32},{32,48},{48,64},{64,80},{80,96},{96,112},{112,128},... | collective-permute-start | bytes 589832 | tf_op jit(solution)/shard_map/ppermute | solution.py:24
  6.8 89.5 %collective-permute-start.1 = (f32[1,24,2048]{2,1,0:T(8,128)}, f32[1,24,2048]{2,1,0:T(8,128)}, u32[]{:S(2)}, u32[]{:S(2)}) collective-permute-start(f32[1,24,2048]{2,1,0:T(8,128)} %get-tuple-element.29), channel_id=1, source_target_pairs={{16,0},{32,16},{48,32},{64,48},{80,64},{96,80},{112,96},{128,112},... | collective-permute-start | bytes 589832 | tf_op jit(solution)/shard_map/ppermute | solution.py:26
  17.8 15.5 %copy-start.3 = (s32[512]{0:T(512)S(1)}, s32[512]{0:T(512)}, u32[]{:S(2)}) copy-start(s32[512]{0:T(512)} %param.17) | copy-start | bytes 6148
  22.9 15.5 %copy-start.15 = (f32[64,512]{1,0:T(8,128)S(1)}, f32[64,512]{1,0:T(8,128)}, u32[]{:S(2)}) copy-start(f32[64,512]{1,0:T(8,128)} %param.19) | copy-start | bytes 393220
  25.5 15.6 %copy-start.2 = (f32[512]{0:T(512)S(1)}, f32[512]{0:T(512)}, u32[]{:S(2)}) copy-start(f32[512]{0:T(512)} %param.18) | copy-start | bytes 6148
  37.1 26.5 %copy-start.29 = (f32[128]{0:T(128)}, f32[128]{0:T(128)S(1)}, u32[]{:S(2)}) copy-start(f32[128]{0:T(128)S(1)} %gather_fusion.3) | copy-start | bytes 1540
  37.1 18.8 %copy-start.16 = (f32[4,8,768]{2,1,0:T(8,128)S(1)}, f32[4,8,768]{2,1,0:T(8,128)}, u32[]{:S(2)}) copy-start(f32[4,8,768]{2,1,0:T(8,128)} %param.14) | copy-start | bytes 294916
  38.4 31.4 %copy-start.26 = (f32[128]{0:T(128)}, f32[128]{0:T(128)S(1)}, u32[]{:S(2)}) copy-start(f32[128]{0:T(128)S(1)} %gather_fusion.10) | copy-start | bytes 1540
  47.3 41.2 %copy-start.23 = (f32[128]{0:T(128)}, f32[128]{0:T(128)S(1)}, u32[]{:S(2)}) copy-start(f32[128]{0:T(128)S(1)} %gather_fusion.17) | copy-start | bytes 1540
  51.6 37.4 %copy-start.20 = (f32[128]{0:T(128)}, f32[128]{0:T(128)S(1)}, u32[]{:S(2)}) copy-start(f32[128]{0:T(128)S(1)} %gather_fusion.25) | copy-start | bytes 1540
  97.5 5.1 collective-permute-start.2
  100.5 6.2 %collective-permute-start.3 = (f32[10,1,2048]{2,0,1:T(8,128)S(1)}, f32[10,1,2048]{2,0,1:T(8,128)S(1)}, u32[]{:S(2)}, u32[]{:S(2)}) collective-permute-start(f32[10,1,2048]{2,0,1:T(8,128)S(1)} %get-tuple-element.27), channel_id=1, source_target_pairs={{1,0},{2,1},{3,2},{4,3},{5,4},{6,5},{7,6},{8,7},{9,8},{10,9},{11,1... | collective-permute-start | bytes 245768 | tf_op jit(solution)/shard_map/ppermute | solution.py:26
  121.2 81.9 %copy-start.6 = (f32[8,24,32,64]{3,2,1,0:T(8,128)}, f32[8,24,32,64]{3,2,1,0:T(8,128)S(1)}, u32[]{:S(2)}) copy-start(f32[8,24,32,64]{3,2,1,0:T(8,128)S(1)} %get-tuple-element.23) | copy-start | bytes 4718596
  121.2 84.4 %copy-start.30 = (f32[128]{0:T(128)S(1)}, f32[128]{0:T(128)}, u32[]{:S(2)}) copy-start(f32[128]{0:T(128)} %copy-done.29) | copy-start | bytes 1540
  121.3 107.7 %copy-start.14 = (f32[128,64]{1,0:T(8,128)S(1)}, f32[128,64]{1,0:T(8,128)}, u32[]{:S(2)}) copy-start(f32[128,64]{1,0:T(8,128)} %gather_fusion.5) | copy-start | bytes 98308
  121.3 107.7 %copy-start.28 = (f32[128]{0:T(128)S(1)}, f32[128]{0:T(128)}, u32[]{:S(2)}) copy-start(f32[128]{0:T(128)} %gather_fusion.4) | copy-start | bytes 1540
  121.3 107.7 %copy-start.34 = (f32[128]{0:T(128)S(1)}, f32[128]{0:T(128)}, u32[]{:S(2)}) copy-start(f32[128]{0:T(128)} %sqrt.28) | copy-start | bytes 1540
  205.5 28.9 %copy-start.4 = (f32[6144,64]{0,1:T(8,128)}, f32[6144,64]{0,1:T(8,128)S(1)}, u32[]{:S(2)}) copy-start(f32[6144,64]{0,1:T(8,128)S(1)} %copy.120) | copy-start | bytes 4718596
  237.4 79.4 %copy-start.27 = (f32[128]{0:T(128)S(1)}, f32[128]{0:T(128)}, u32[]{:S(2)}) copy-start(f32[128]{0:T(128)} %copy-done.26) | copy-start | bytes 1540
  237.4 102.8 %copy-start.13 = (f32[128,64]{1,0:T(8,128)S(1)}, f32[128,64]{1,0:T(8,128)}, u32[]{:S(2)}) copy-start(f32[128,64]{1,0:T(8,128)} %gather_fusion.12) | copy-start | bytes 98308
  237.4 102.8 %copy-start.25 = (f32[128]{0:T(128)S(1)}, f32[128]{0:T(128)}, u32[]{:S(2)}) copy-start(f32[128]{0:T(128)} %gather_fusion.11) | copy-start | bytes 1540
  237.4 102.8 %copy-start.33 = (f32[128]{0:T(128)S(1)}, f32[128]{0:T(128)}, u32[]{:S(2)}) copy-start(f32[128]{0:T(128)} %sqrt.29) | copy-start | bytes 1540
  348.8 78.8 %copy-start.24 = (f32[128]{0:T(128)S(1)}, f32[128]{0:T(128)}, u32[]{:S(2)}) copy-start(f32[128]{0:T(128)} %copy-done.23) | copy-start | bytes 1540
  348.8 102.1 %copy-start.12 = (f32[128,64]{1,0:T(8,128)S(1)}, f32[128,64]{1,0:T(8,128)}, u32[]{:S(2)}) copy-start(f32[128,64]{1,0:T(8,128)} %gather_fusion.19) | copy-start | bytes 98308
  348.8 102.1 %copy-start.22 = (f32[128]{0:T(128)S(1)}, f32[128]{0:T(128)}, u32[]{:S(2)}) copy-start(f32[128]{0:T(128)} %gather_fusion.18) | copy-start | bytes 1540
  348.8 102.1 %copy-start.32 = (f32[128]{0:T(128)S(1)}, f32[128]{0:T(128)}, u32[]{:S(2)}) copy-start(f32[128]{0:T(128)} %sqrt.30) | copy-start | bytes 1540
  459.4 79.3 %copy-start.21 = (f32[128]{0:T(128)S(1)}, f32[128]{0:T(128)}, u32[]{:S(2)}) copy-start(f32[128]{0:T(128)} %copy-done.20) | copy-start | bytes 1540
  459.4 102.6 %copy-start.11 = (f32[128,64]{1,0:T(8,128)S(1)}, f32[128,64]{1,0:T(8,128)}, u32[]{:S(2)}) copy-start(f32[128,64]{1,0:T(8,128)} %gather_fusion.27) | copy-start | bytes 98308
  459.4 102.6 %copy-start.19 = (f32[128]{0:T(128)S(1)}, f32[128]{0:T(128)}, u32[]{:S(2)}) copy-start(f32[128]{0:T(128)} %gather_fusion.26) | copy-start | bytes 1540
  459.4 102.6 %copy-start.31 = (f32[128]{0:T(128)S(1)}, f32[128]{0:T(128)}, u32[]{:S(2)}) copy-start(f32[128]{0:T(128)} %sqrt.31) | copy-start | bytes 1540
  (7 other events, 32.9 us)
where the time goes:
time: 586 us; the launch traced here: 575 us
  blocking collectives  303 us (52%)
  other arithmetic  115 us (20%)
  local copies, waits for them, and re-layouts  104 us (18%)
  matrix products  35.6 us (6%)
  starting transfers between devices  11.3 us (2%)
    psum x4, blocking collectives, body(): lax.psum(jnp.where(inside[None, :], jnp.take(analysis, flat_index, axis=1...  303 us
    another operation x12, other arithmetic, solve_batch(): factor = jnp.linalg.cholesky(covariance)  49.6 us
    another operation x8, other arithmetic, solve_batch(): solved = jax.scipy.linalg.cho_solve((factor, True), innovation.T)  41.8 us
    mul x4, local copies, waits for them, and re-layouts, body(): across[:, :, :, None] * vertical[:, None, None, :]  26.6 us
    dot_general x4, matrix products, body(): jnp.dot(anomaly.T, centred, precision=HIGHEST) / (MEM - 1) * loc_taper  19.2 us
    dot_general x4, matrix products, body(): analysis = analysis + jnp.dot(gain_rows, link, precision=HIGHEST)  12.7 us
  transfers between devices with their start and end apart: 4, of which 2 were waited for; matrix products, arithmetic and copies ran while one was open for 15% of the time, Pallas kernels for 0%

commit v1 on v0

v1 whole, which is shorter than its diff:
```python
import functools
import jax
import jax.numpy as jnp
from jax import lax
from jax.experimental import pallas as pl
from jax.experimental.pallas import tpu as pltpu
from jax.sharding import PartitionSpec as P

MEM = 64
LEV = 32
OBS_B = 128
NBATCH = 4
HIGHEST = lax.Precision.HIGHEST
F32 = jnp.float32
BF16 = jnp.bfloat16


def dot(a, b, precision=None):
    return jnp.dot(a, b, preferred_element_type=F32, precision=precision)


def dot_nt(a, b, precision=None):
    return lax.dot_general(
        a, b, (((1,), (1,)), ((), ())), preferred_element_type=F32, precision=precision
    )


def split(value):
    high = value.astype(BF16)
    return high, (value - high.astype(F32)).astype(BF16)


def eliminate_four(rows, first):
    blocks = len(rows)
    shape = (8, 128)
    columns = [
        [jnp.broadcast_to(rows[v][0][:, first + j : first + j + 1], shape) for v in range(blocks)]
        for j in range(4)
    ]

    def entry(i, j):
        return jnp.broadcast_to(columns[j][0][first + i : first + i + 1, :], shape)

    a00, a01, a11 = entry(0, 0), entry(0, 1), entry(1, 1)
    a20, a21, a30, a31 = entry(2, 0), entry(2, 1), entry(3, 0), entry(3, 1)
    a22, a32, a33 = entry(2, 2), entry(3, 2), entry(3, 3)
    inv = 1.0 / (a00 * a11 - a01 * a01)
    p00, p01, p11 = a11 * inv, -a01 * inv, a00 * inv
    x20, x21 = a20 * p00 + a21 * p01, a20 * p01 + a21 * p11
    x30, x31 = a30 * p00 + a31 * p01, a30 * p01 + a31 * p11
    s22 = a22 - (x20 * a20 + x21 * a21)
    s32 = a32 - (x30 * a20 + x31 * a21)
    s33 = a33 - (x30 * a30 + x31 * a31)
    inv = 1.0 / (s22 * s33 - s32 * s32)
    q22, q32, q33 = s33 * inv, -s32 * inv, s22 * inv
    lane_row = lax.broadcasted_iota(jnp.int32, shape, 0)
    result = [[None] * len(rows[0]) for _ in range(blocks)]
    for col in range(len(rows[0])):
        r0, r1, r2, r3 = (
            jnp.broadcast_to(rows[0][col][first + i : first + i + 1, :], shape) for i in range(4)
        )
        t2 = r2 - (x20 * r0 + x21 * r1)
        t3 = r3 - (x30 * r0 + x31 * r1)
        n2 = q22 * t2 + q32 * t3
        n3 = q32 * t2 + q33 * t3
        n0 = p00 * r0 + p01 * r1 - (x20 * n2 + x30 * n3)
        n1 = p01 * r0 + p11 * r1 - (x21 * n2 + x31 * n3)
        for v in range(blocks):
            value = rows[v][col] - (
                (columns[0][v] * n0 + columns[1][v] * n1)
                + (columns[2][v] * n2 + columns[3][v] * n3)
            )
            if v == 0:
                value = jnp.where(lane_row == first, n0, value)
                value = jnp.where(lane_row == first + 1, n1, value)
                value = jnp.where(lane_row == first + 2, n2, value)
                value = jnp.where(lane_row == first + 3, n3, value)
            result[v][col] = value
    return result


def eliminate_eight(rows):
    rows = eliminate_four(rows, 0)
    rows = eliminate_four(rows, 4)
    rows = [[pltpu.roll(row[0], 120, 1)] + row[1:] for row in rows]
    return rows[1:] + rows[:1]


def flat(rows):
    return tuple(value for row in rows for value in row)


def nested(values, width):
    return [list(values[i : i + width]) for i in range(0, len(values), width)]


def taper_of(dx, dy, dl, radius):
    across = jnp.maximum(1.0 - (dx * dx + dy * dy) / (radius * radius), 0.0)
    return across * across, 1.0 + (dl * 0.125) * (dl * 0.125)


def analysis_kernel(
    axes, f_ref, p_ref, rows_ref, cols_ref, o_ref, state_ref, near_ref, w1_ref, w2_ref, hor_ref, ver_ref
):
    cells = f_ref.shape[0]
    start_x, start_y = axes()
    packed = p_ref[...].T
    state_ref[:, 0:256] = packed[:MEM]
    state_ref[:, 256:512] = packed[MEM:]

    def row_of(index, batch):
        return rows_ref[index : index + 1, batch * OBS_B : (batch + 1) * OBS_B]

    def solve_begin(batch):
        low = batch * OBS_B
        prior = state_ref[:, low : low + OBS_B]
        anomaly = prior - jnp.mean(prior, axis=0, keepdims=True)
        variance = row_of(5, batch)
        deviation = jnp.sqrt(variance)
        inv_dev = 1.0 / deviation
        noise = rows_ref[8:72, low : low + OBS_B]
        innovation = row_of(4, batch) + deviation * noise - prior
        scaled = anomaly * (inv_dev * (1.0 / (MEM - 1) ** 0.5))
        both = jnp.concatenate([scaled, innovation * inv_dev], axis=0)
        right = jnp.concatenate([scaled, jnp.zeros((64, OBS_B), F32)], axis=0)
        product = dot_nt(both, right, HIGHEST)
        eye = lax.broadcasted_iota(jnp.int32, (64, 128), 0) == lax.broadcasted_iota(jnp.int32, (64, 128), 1)
        system = product[:64] + eye.astype(F32)
        rhs = scaled * inv_dev
        rows = [[system[8 * v : 8 * v + 8], rhs[8 * v : 8 * v + 8]] for v in range(8)]
        return anomaly, innovation * variance_inverse(inv_dev), product[64:, :64], rows

    def variance_inverse(inv_dev):
        return inv_dev * inv_dev

    def near(batch, anomaly):
        low, high = batch * OBS_B, (batch + 1) * OBS_B
        if batch == NBATCH - 1:
            return
        links = dot(anomaly.T, state_ref[:, high:], HIGHEST)
        for later in range(batch + 1, NBATCH):
            cut = slice(later * OBS_B, (later + 1) * OBS_B)
            across, down = taper_of(
                cols_ref[low:high, 0:1] - rows_ref[0:1, cut],
                cols_ref[low:high, 1:2] - rows_ref[1:2, cut],
                cols_ref[low:high, 2:3] - rows_ref[2:3, cut],
                cols_ref[low:high, 3:4],
            )
            at = (later - batch - 1) * OBS_B
            near_ref[:, at : at + OBS_B] = links[:, at : at + OBS_B] * (across / (down * (MEM - 1)))

    def tile_begin(batch, anomaly, gain):
        zero = jnp.zeros((64, 128), BF16)
        high, low = split(anomaly)
        high_two = jnp.concatenate(
            [jnp.concatenate([high, zero], axis=1), jnp.concatenate([zero, high], axis=1)], axis=0
        )
        w1_ref[0:128, :] = high_two
        w1_ref[128:256, :] = high_two
        w1_ref[256:384, :] = jnp.concatenate(
            [jnp.concatenate([low, zero], axis=1), jnp.concatenate([zero, low], axis=1)], axis=0
        )
        turned = gain.T
        high, low = split(turned)
        zero = jnp.zeros((128, 64), BF16)
        w2_ref[:, 0:128] = jnp.concatenate(
            [jnp.concatenate([high, zero], axis=1), jnp.concatenate([zero, high], axis=1)], axis=0
        )
        w2_ref[:, 128:256] = jnp.concatenate(
            [jnp.concatenate([low, zero], axis=1), jnp.concatenate([zero, low], axis=1)], axis=0
        )
        cell = lax.broadcasted_iota(jnp.int32, (cells, 1), 0)
        level = lax.broadcasted_iota(jnp.int32, (LEV, 1), 0).astype(F32)
        cell_x = (cell // 24 + start_x).astype(F32)
        cell_y = (cell % 24 + start_y).astype(F32)
        across, down = taper_of(
            cell_x - row_of(0, batch), cell_y - row_of(1, batch), level - row_of(2, batch), row_of(3, batch)
        )
        hor_ref[...] = across
        ver_ref[...] = 1.0 / (down * (MEM - 1))

    def tile_step(src_ref, step):
        lanes = [pl.ds(pl.multiple_of(step * 256 + 128 * h, 128), 128) for h in range(2)]
        state = jnp.concatenate([src_ref[:, lanes[0]], src_ref[:, lanes[1]]], axis=0)
        high, low = split(state)
        link = dot(jnp.concatenate([high, low], axis=1), w1_ref[0:256, :]) + dot(high, w1_ref[256:384, :])
        parts = []
        for h in range(2):
            sides = []
            for p in range(2):
                down = ver_ref[pl.ds(4 * step + 2 * h + p, 1), :]
                sides.append(
                    link[h * cells : (h + 1) * cells, p * 128 : p * 128 + 128] * hor_ref[...] * down
                )
            parts.append(jnp.concatenate(sides, axis=1))
        high, low = split(jnp.concatenate(parts, axis=0))
        wide = dot(high, w2_ref[...])
        state = state + (wide[:, :128] + wide[:, 128:] + dot(low, w2_ref[:, 0:128]))
        for h in range(2):
            o_ref[:, lanes[h]] = state[h * cells : (h + 1) * cells]

    for batch in range(NBATCH + 1):
        if batch < NBATCH:
            anomaly, direct, cross, rows = solve_begin(batch)
            near(batch, anomaly)
            values = flat(rows)
        else:
            values = ()

        def step_body(step, values):
            if batch > 0:
                tile_step(f_ref if batch == 1 else o_ref, step)
            if batch < NBATCH:
                values = flat(eliminate_eight(nested(values, 2)))
            return values

        values = lax.fori_loop(0, 8, step_body, values)
        if batch < NBATCH:
            solved = jnp.concatenate([row[1] for row in nested(values, 2)], axis=0)
            gain = direct - dot(cross, solved, HIGHEST)
            if batch < NBATCH - 1:
                high = (batch + 1) * OBS_B
                state_ref[:, high:] = state_ref[:, high:] + dot(
                    gain, near_ref[:, : NBATCH * OBS_B - high], HIGHEST
                )
            tile_begin(batch, anomaly, gain)


def analyse(axes, forecast, packed, rows, cols):
    cells = forecast.shape[0]
    return pl.pallas_call(
        functools.partial(analysis_kernel, axes),
        out_shape=jax.ShapeDtypeStruct(forecast.shape, F32),
        in_specs=[pl.BlockSpec(memory_space=pltpu.VMEM)] * 4,
        out_specs=pl.BlockSpec(memory_space=pltpu.VMEM),
        scratch_shapes=[
            pltpu.VMEM((MEM, NBATCH * OBS_B), F32),
            pltpu.VMEM((OBS_B, (NBATCH - 1) * OBS_B), F32),
            pltpu.VMEM((384, 256), BF16),
            pltpu.VMEM((256, 256), BF16),
            pltpu.VMEM((cells, OBS_B), F32),
            pltpu.VMEM((LEV, OBS_B), F32),
        ],
        compiler_params=pltpu.CompilerParams(vmem_limit_bytes=48 * 1024 * 1024),
        name="analysis",
    )(forecast, packed, rows, cols)


MESH = pl.DeviceIdType.MESH


def forecast_kernel(
    n_x, n_y,
    ens_ref, w_ref, cell_ref, batch_ref, radius_ref, value_ref, var_ref, noise_ref,
    f_ref, p_ref, rows_ref, cols_ref,
    west_ref, east_ref, south_ref, north_ref, first_ref, last_ref,
    data_ref, spread_ref, pick_ref, found_ref,
    part_ref, got_y_ref, sum_ref, got_x_ref, total_ref, all_ref,
    halo_send, halo_recv, send_1, recv_1, send_2, recv_2, send_3, recv_3,
):
    gx, gy = lax.axis_index("gx"), lax.axis_index("gy")
    rows_x, rows_y = ens_ref.shape[0], ens_ref.shape[1]
    cells = rows_x * rows_y

    def peer(axis, index, count, step):
        return {axis: lax.rem(index + step, count)}

    barrier = pltpu.get_barrier_semaphore()
    for step in range(1, n_x):
        pl.semaphore_signal(barrier, inc=1, device_id=peer("gx", gx, n_x, step), device_id_type=MESH)
    for step in range(1, n_y):
        pl.semaphore_signal(barrier, inc=1, device_id=peer("gy", gy, n_y, step), device_id_type=MESH)

    for x in range(rows_x):
        first_ref[x : x + 1, :] = ens_ref[x, 0:1, :]
        last_ref[x : x + 1, :] = ens_ref[x, rows_y - 1 : rows_y, :]

    pl.semaphore_wait(barrier, n_x + n_y - 2)

    def halo(slot, src, dst, axis, target):
        return pltpu.make_async_remote_copy(
            src_ref=src, dst_ref=dst, send_sem=halo_send.at[slot], recv_sem=halo_recv.at[slot],
            device_id={axis: target}, device_id_type=MESH,
        )

    copies = (
        (halo(0, ens_ref.at[rows_x - 1], west_ref, "gx", lax.rem(gx + 1, n_x)), gx < n_x - 1, gx > 0, west_ref),
        (halo(1, ens_ref.at[0], east_ref, "gx", lax.rem(gx + n_x - 1, n_x)), gx > 0, gx < n_x - 1, east_ref),
        (halo(2, last_ref, south_ref, "gy", lax.rem(gy + 1, n_y)), gy < n_y - 1, gy > 0, south_ref),
        (halo(3, first_ref, north_ref, "gy", lax.rem(gy + n_y - 1, n_y)), gy > 0, gy < n_y - 1, north_ref),
    )
    for copy, sends, _, _ in copies:
        pl.when(sends)(copy.start)

    data_ref[...] = jnp.zeros(data_ref.shape, F32)
    data_ref[0:3, :] = cell_ref[...].astype(F32)
    data_ref[3:4, :] = radius_ref[...].astype(F32)
    data_ref[4:5, :] = value_ref[...]
    data_ref[5:6, :] = var_ref[...]
    data_ref[8:72, :] = noise_ref[...]
    n_obs = batch_ref.shape[1]
    square = (n_obs, n_obs)
    at_row, at_lane = lax.broadcasted_iota(jnp.int32, square, 0), lax.broadcasted_iota(jnp.int32, square, 1)
    before = (at_row < at_lane).astype(F32).astype(BF16)
    kind = lax.broadcasted_iota(jnp.int32, (8, n_obs), 0)
    same = (kind == batch_ref[...]).astype(F32)
    count = dot(same.astype(BF16), before)
    rank = jnp.sum(same * (count + (kind * OBS_B).astype(F32)), axis=0, keepdims=True)
    chosen = (at_row.astype(F32) == rank).astype(F32).astype(BF16)
    data = data_ref[...]
    high = data.astype(BF16)
    rest = data - high.astype(F32)
    middle, low = split(rest)
    thirds = dot_nt(chosen, jnp.concatenate([high, middle, low], axis=0))
    table = (thirds[:, 0:128] + thirds[:, 128:256]) + thirds[:, 256:384]
    cols_ref[...] = table[:, 0:8]
    rows_ref[...] = table.T[0:72]
    obs_x = table[:, 0:1] - (gx * rows_x).astype(F32)
    obs_y = table[:, 1:2] - (gy * rows_y).astype(F32)
    inside = (obs_x >= 0.0) & (obs_x < rows_x) & (obs_y >= 0.0) & (obs_y < rows_y)
    place = jnp.where(inside, obs_x * rows_y + obs_y, -1.0)
    pick_ref[...] = (
        lax.broadcasted_iota(jnp.int32, pick_ref.shape, 1).astype(F32) == place
    ).astype(F32).astype(BF16)
    obs_l = table[:, 2:3]
    pair = jnp.floor(obs_l * 0.5)
    odd = obs_l - 2.0 * pair

    for k in range(4):
        for y in range(rows_y):
            block = w_ref[k, :, 128 * (y // 4) : 128 * (y // 4) + 128]
            if y % 4:
                block = pltpu.roll(block, 128 - 32 * (y % 4), 1)
            spread_ref[pl.ds(k * cells + y, rows_x, stride=rows_y), :] = block
    found_ref[...] = jnp.zeros(found_ref.shape, F32)

    for copy, _, receives, halo_ref in copies:
        pl.when(receives)(copy.wait_recv)

        @pl.when(jnp.logical_not(receives))
        def _():
            halo_ref[...] = jnp.zeros(halo_ref.shape, F32)

    def forecast_step(step, carry):
        lanes = pl.ds(pl.multiple_of(step * 256, 256), 256)
        level = lax.broadcasted_iota(jnp.int32, (128, 256), 0)
        column = lax.broadcasted_iota(jnp.int32, (128, 256), 1) // 64 + 4 * step
        ones = (level == column).astype(F32).astype(BF16)
        high, low = split(spread_ref[...])
        weights = dot(jnp.concatenate([high, low], axis=1), jnp.concatenate([ones, ones], axis=0))
        side = lax.broadcasted_iota(jnp.int32, (rows_y, 256), 0)
        parts = []
        for x in range(rows_x):
            q = ens_ref[x, :, lanes]
            west = west_ref[:, lanes] if x == 0 else ens_ref[x - 1, :, lanes]
            east = east_ref[:, lanes] if x == rows_x - 1 else ens_ref[x + 1, :, lanes]
            south = jnp.where(side == 0, south_ref[x : x + 1, lanes], pltpu.roll(q, 1, 0))
            north = jnp.where(side == rows_y - 1, north_ref[x : x + 1, lanes], pltpu.roll(q, rows_y - 1, 0))
            total = q
            for k, other in enumerate((west, east, south, north)):
                at = k * cells + x * rows_y
                total = total + weights[at : at + rows_y] * (other - q)
            parts.append(total)
        step_rows = jnp.concatenate(parts, axis=0)
        f_ref[:, lanes] = step_rows
        high, low = split(step_rows)
        here = dot(pick_ref[:, 0:cells], high) + dot(pick_ref[:, 0:cells], low)
        found = found_ref[...]
        for h in range(2):
            found = found + jnp.where(
                pair == (2 * step + h).astype(F32), here[:, h * 128 : h * 128 + 128], 0.0
            )
        found_ref[...] = found
        return carry

    lax.fori_loop(0, 8, forecast_step, 0)
    found = found_ref[...]
    turned = pltpu.roll(found, 64, 1)
    left = jnp.where(odd == 0.0, found, turned)
    right = jnp.where(odd == 0.0, turned, found)
    half = n_obs // 2
    lane = lax.broadcasted_iota(jnp.int32, (half, 128), 1)
    part_ref[...] = jnp.where(lane < 64, left[:half], right[half:])

    share = half // n_y

    def send(step, axis, index, count, src, dst, sends, recvs):
        return pltpu.make_async_remote_copy(
            src_ref=src, dst_ref=dst, send_sem=sends.at[step], recv_sem=recvs.at[step],
            device_id=peer(axis, index, count, step), device_id_type=MESH,
        )

    def rows_of(index):
        return pl.ds(pl.multiple_of(index * share, share), share)

    first = [
        send(s, "gy", gy, n_y, part_ref.at[rows_of(lax.rem(gy + s, n_y))], got_y_ref.at[s], send_1, recv_1)
        for s in range(1, n_y)
    ]
    for copy in first:
        copy.start()
    total = part_ref[rows_of(gy), :]
    for s, copy in enumerate(first, 1):
        copy.wait_recv()
        total = total + got_y_ref[s]
    sum_ref[...] = total
    second = [send(s, "gx", gx, n_x, sum_ref, got_x_ref.at[s], send_2, recv_2) for s in range(1, n_x)]
    for copy in second:
        copy.start()
    for s, copy in enumerate(second, 1):
        copy.wait_recv()
        total = total + got_x_ref[s]
    total_ref[...] = total
    third = [
        send(s, "gy", gy, n_y, total_ref, all_ref.at[rows_of(gy)], send_3, recv_3) for s in range(1, n_y)
    ]
    for copy in third:
        copy.start()
    all_ref[rows_of(gy), :] = total
    for copy, sends, _, _ in copies:
        pl.when(sends)(copy.wait_send)
    for copy in first + second:
        copy.wait_send()
    for copy in third:
        copy.wait_recv()
    p_ref[...] = all_ref[...]
    for copy in third:
        copy.wait_send()


def forecast_and_gather(n_x, n_y, ensemble, weights, obs_cell, obs_batch, obs_radius, obs_value, obs_noise, obs_var):
    rows_x, rows_y, width = ensemble.shape
    cells = rows_x * rows_y
    n_obs = obs_batch.shape[0]
    share = n_obs // 2 // n_y
    vmem = pl.BlockSpec(memory_space=pltpu.VMEM)
    dma = pltpu.SemaphoreType.DMA
    return pl.pallas_call(
        functools.partial(forecast_kernel, n_x, n_y),
        out_shape=(
            jax.ShapeDtypeStruct((cells, width), F32),
            jax.ShapeDtypeStruct((n_obs // 2, 128), F32),
            jax.ShapeDtypeStruct((72, n_obs), F32),
            jax.ShapeDtypeStruct((n_obs, 8), F32),
        ),
        in_specs=[vmem] * 8,
        out_specs=(vmem,) * 4,
        scratch_shapes=[
            pltpu.VMEM((rows_y, width), F32),
            pltpu.VMEM((rows_y, width), F32),
            pltpu.VMEM((rows_x, width), F32),
            pltpu.VMEM((rows_x, width), F32),
            pltpu.VMEM((rows_x, width), F32),
            pltpu.VMEM((rows_x, width), F32),
            pltpu.VMEM((128, n_obs), F32),
            pltpu.VMEM((4 * cells, 128), F32),
            pltpu.VMEM((n_obs, 256), BF16),
            pltpu.VMEM((n_obs, 128), F32),
            pltpu.VMEM((n_obs // 2, 128), F32),
            pltpu.VMEM((n_y, share, 128), F32),
            pltpu.VMEM((share, 128), F32),
            pltpu.VMEM((n_x, share, 128), F32),
            pltpu.VMEM((share, 128), F32),
            pltpu.VMEM((n_obs // 2, 128), F32),
            dma((4,)), dma((4,)),
            dma((n_y,)), dma((n_y,)), dma((n_x,)), dma((n_x,)), dma((n_y,)), dma((n_y,)),
        ],
        compiler_params=pltpu.CompilerParams(
            collective_id=0, has_side_effects=True, vmem_limit_bytes=48 * 1024 * 1024
        ),
        name="forecast_and_gather",
    )(
        ensemble, weights, obs_cell, obs_batch.reshape(1, n_obs), obs_radius.reshape(1, n_obs),
        obs_value.reshape(1, n_obs), obs_var.reshape(1, n_obs), obs_noise,
    )


def solution(mesh):
    n_x, n_y = mesh.shape["gx"], mesh.shape["gy"]

    def body(ensemble, *rest):
        rows_x, rows_y, width = ensemble.shape
        forecast, packed, rows, cols = forecast_and_gather(n_x, n_y, ensemble, *rest)
        analysis = analyse(
            lambda: (lax.axis_index("gx") * rows_x, lax.axis_index("gy") * rows_y), forecast, packed, rows, cols
        )
        return analysis.reshape(rows_x, rows_y, width)

    placed = (P("gx", "gy", None), P(None, "gx", "gy"), P(), P(), P(), P(), P(), P())
    return jax.shard_map(
        body, mesh=mesh, in_specs=placed, out_specs=P("gx", "gy", None), check_vma=False
    )
```

time: 586 us -> 70.8 us (0.12); the launches traced: 575 us -> 70.5 us
  blocking collectives: 303 us -> 0 us
  other arithmetic: 115 us -> 0 us
  local copies, waits for them, and re-layouts: 104 us -> 6.62 us
  Pallas kernels: 0 us -> 63.8 us
  matrix products: 35.6 us -> 0 us
  starting transfers between devices: 11.3 us -> 0 us
    psum x4 -> x0, blocking collectives: 303 us -> none  [body(): lax.psum(jnp.where(inside[None, :], jnp.take(analysis, flat_index, axis=1...]
    another operation x20 -> x0, other arithmetic: 91.4 us -> none  [the longest x12 49.6 us: solve_batch(): factor = jnp.linalg.cholesky(covariance)]
    pallas_call x0 -> x2, Pallas kernels: none -> 63.8 us  [the longest x1 37.9 us: forecast_and_gather(): pl.pallas_call(functools.partial(forecast_kernel, n_x, n_y), out_shape=(j...]
    gather x32 -> x0, local copies, waits for them, and re-layouts: 45.8 us -> none  [the longest x4 8.24 us: body(): jnp.take(analysis, flat_index, axis=1)]
    dot_general x12 -> x0, matrix products: 33.3 us -> none  [the longest x4 19.2 us: body(): jnp.dot(anomaly.T, centred, precision=HIGHEST) / (MEM - 1) * loc_taper]
    mul x8 -> x0, local copies, waits for them, and re-layouts: 28.2 us -> none  [the longest x4 26.6 us: body(): across[:, :, :, None] * vertical[:, None, None, :]]
    ppermute x4 -> x0, starting transfers between devices: 11.3 us -> none  [the longest x2 7.89 us: padded_2(): lax.ppermute(tail, axis, [(i, (i + 1) % count) for i in range(ends)])]
    reduce_sum x5 -> x0, other arithmetic: 10 us -> none  [the longest x1 9.61 us: body(): centred = analysis - jnp.mean(analysis, axis=0, keepdims=True)]
  transfers between devices with their start and end apart: 4 -> 0, of which waited for: 2 -> 0; matrix products, arithmetic and copies ran while one was open for 15% -> 0% of each run, Pallas kernels for 0% -> 0%
where the time goes in v1:
time: 70.8 us; the launch traced here: 70.5 us
  Pallas kernels  63.8 us (90%)
  local copies, waits for them, and re-layouts  6.62 us (9%)
    pallas_call x1, Pallas kernels, forecast_and_gather(): pl.pallas_call(functools.partial(forecast_kernel, n_x, n_y), out_shape=(j...  37.9 us
    pallas_call x1, Pallas kernels, analyse(): pl.pallas_call(functools.partial(analysis_kernel, axes), out_shape=jax.Sh...  26 us
    unnamed x16, local copies, waits for them, and re-layouts  6.62 us

profile of v1, /device:TPU:1, one launch (start us, length us, event | category | flops | bytes accessed | tf_op | source)
XLA Modules:
  0.0 70.5 jit_solution(7522048217132215594)
XLA Ops:
  0.0 0.0 copy-start
  0.0 1.4 %copy-done = f32[8,24,2048]{2,1,0:T(8,128)S(1)} copy-done((f32[8,24,2048]{2,1,0:T(8,128)S(1)}, f32[8,24,2048]{2,1,0:T(8,128)}, u32[]{:S(2)}) %copy-start) | copy-done | bytes 1572888
  1.4 0.0 copy-start.1
  1.4 0.9 %copy-done.1 = f32[64,512]{1,0:T(8,128)S(1)} copy-done((f32[64,512]{1,0:T(8,128)S(1)}, f32[64,512]{1,0:T(8,128)}, u32[]{:S(2)}) %copy-start.1) | copy-done | bytes 131096
  2.3 0.0 copy-start.2
  2.3 0.9 %copy-done.2 = f32[4,8,768]{2,1,0:T(8,128)S(1)} copy-done((f32[4,8,768]{2,1,0:T(8,128)S(1)}, f32[4,8,768]{2,1,0:T(8,128)}, u32[]{:S(2)}) %copy-start.2) | copy-done | bytes 98328
  3.2 0.0 copy-start.3
  3.2 0.7 copy-done.3
  3.9 0.0 copy-start.4
  3.9 0.7 copy-done.4
  4.6 0.0 copy-start.5
  4.6 0.7 copy-done.5
  5.3 0.0 copy-start.6
  5.3 0.7 copy-done.6
  6.0 0.0 copy-start.7
  6.0 0.7 copy-done.7
  6.6 37.9 %forecast_and_gather.1 = (f32[192,2048]{1,0:T(8,128)S(1)}, f32[256,128]{1,0:T(8,128)S(1)}, f32[72,512]{1,0:T(8,128)S(1)}, f32[512,8]{1,0:T(8,128)S(1)}) custom-call(f32[8,24,2048]{2,1,0:T(8,128)S(1)} %copy-done, f32[4,8,768]{2,1,0:T(8,128)S(1)} %copy-done.2, s32[3,512]{1,0:T(4,128)S(1)} %copy-done.3, s32[1,512]{1,0:T(1,128)S(1)} %bitcast.5, ...), custom_call_target="tpu_custom_call" | custom-call | tf_op jit(solution)/shard_map/forecast_and_gather/pallas_call | solution.py:438
  44.5 26.0 %analysis.1 = f32[192,2048]{1,0:T(8,128)} custom-call(f32[192,2048]{1,0:T(8,128)S(1)} %get-tuple-element.9.f_ref, f32[256,128]{1,0:T(8,128)S(1)} %get-tuple-element.10.p_ref, f32[72,512]{1,0:T(8,128)S(1)} %get-tuple-element.11.rows_ref, f32[512,8]{1,0:T(8,128)S(1)} %get-tuple-element.12.cols_ref), custom_call_target="tpu_custom_call" | custom-call | tf_op jit(solution)/shard_map/analysis/pallas_call | solution.py:231
Async XLA Ops:
  0.0 1.4 %copy-start = (f32[8,24,2048]{2,1,0:T(8,128)S(1)}, f32[8,24,2048]{2,1,0:T(8,128)}, u32[]{:S(2)}) copy-start(f32[8,24,2048]{2,1,0:T(8,128)} %ens_ref.1) | copy-start | bytes 4718596
  1.4 0.9 %copy-start.1 = (f32[64,512]{1,0:T(8,128)S(1)}, f32[64,512]{1,0:T(8,128)}, u32[]{:S(2)}) copy-start(f32[64,512]{1,0:T(8,128)} %noise_ref.1) | copy-start | bytes 393220
  2.3 0.9 %copy-start.2 = (f32[4,8,768]{2,1,0:T(8,128)S(1)}, f32[4,8,768]{2,1,0:T(8,128)}, u32[]{:S(2)}) copy-start(f32[4,8,768]{2,1,0:T(8,128)} %w_ref.1) | copy-start | bytes 294916
  3.2 0.7 copy-start.3
  3.9 0.7 copy-start.4
  4.6 0.7 copy-start.5
  5.3 0.7 copy-start.6
  6.0 0.7 copy-start.7

commit v2 on v1

--- a/solution.py
+++ b/solution.py
@@ -251,19 +251,41 @@
 
 def forecast_kernel(
     n_x, n_y,
-    ens_ref, w_ref, cell_ref, batch_ref, radius_ref, value_ref, var_ref, noise_ref,
+    ens_hbm, w_hbm, cell_hbm, batch_hbm, radius_hbm, value_hbm, var_hbm, noise_hbm,
     f_ref, p_ref, rows_ref, cols_ref,
+    ens_ref, w_ref, cell_ref, batch_ref, ints_ref, floats_ref,
     west_ref, east_ref, south_ref, north_ref, first_ref, last_ref,
-    data_ref, spread_ref, pick_ref, found_ref,
+    data_ref, spread_ref, point_ref, mix_ref, edge_ref, found_ref,
     part_ref, got_y_ref, sum_ref, got_x_ref, total_ref, all_ref,
-    halo_send, halo_recv, send_1, recv_1, send_2, recv_2, send_3, recv_3,
+    loads, halo_send, halo_recv, send_1, recv_1, send_2, recv_2, send_3, recv_3,
 ):
     gx, gy = lax.axis_index("gx"), lax.axis_index("gy")
     rows_x, rows_y = ens_ref.shape[0], ens_ref.shape[1]
     cells = rows_x * rows_y
+    n_obs = batch_ref.shape[1]
 
     def peer(axis, index, count, step):
         return {axis: lax.rem(index + step, count)}
+
+    small = [
+        pltpu.make_async_copy(src, dst, loads.at[i])
+        for i, (src, dst) in enumerate(
+            (
+                (batch_hbm, batch_ref),
+                (cell_hbm, cell_ref),
+                (noise_hbm, data_ref.at[8:72]),
+                (radius_hbm, ints_ref),
+                (value_hbm, floats_ref.at[0]),
+                (var_hbm, floats_ref.at[1]),
+            )
+        )
+    ]
+    load_weights = pltpu.make_async_copy(w_hbm, w_ref, loads.at[6])
+    load_tile = pltpu.make_async_copy(ens_hbm, ens_ref, loads.at[7])
+    for copy in small:
+        copy.start()
+    load_tile.start()
+    load_weights.start()
 
     barrier = pltpu.get_barrier_semaphore()
     for step in range(1, n_x):
@@ -271,34 +293,14 @@
     for step in range(1, n_y):
         pl.semaphore_signal(barrier, inc=1, device_id=peer("gy", gy, n_y, step), device_id_type=MESH)
 
-    for x in range(rows_x):
-        first_ref[x : x + 1, :] = ens_ref[x, 0:1, :]
-        last_ref[x : x + 1, :] = ens_ref[x, rows_y - 1 : rows_y, :]
-
-    pl.semaphore_wait(barrier, n_x + n_y - 2)
-
-    def halo(slot, src, dst, axis, target):
-        return pltpu.make_async_remote_copy(
-            src_ref=src, dst_ref=dst, send_sem=halo_send.at[slot], recv_sem=halo_recv.at[slot],
-            device_id={axis: target}, device_id_type=MESH,
-        )
-
-    copies = (
-        (halo(0, ens_ref.at[rows_x - 1], west_ref, "gx", lax.rem(gx + 1, n_x)), gx < n_x - 1, gx > 0, west_ref),
-        (halo(1, ens_ref.at[0], east_ref, "gx", lax.rem(gx + n_x - 1, n_x)), gx > 0, gx < n_x - 1, east_ref),
-        (halo(2, last_ref, south_ref, "gy", lax.rem(gy + 1, n_y)), gy < n_y - 1, gy > 0, south_ref),
-        (halo(3, first_ref, north_ref, "gy", lax.rem(gy + n_y - 1, n_y)), gy > 0, gy < n_y - 1, north_ref),
-    )
-    for copy, sends, _, _ in copies:
-        pl.when(sends)(copy.start)
-
-    data_ref[...] = jnp.zeros(data_ref.shape, F32)
+    for copy in small:
+        copy.wait()
     data_ref[0:3, :] = cell_ref[...].astype(F32)
-    data_ref[3:4, :] = radius_ref[...].astype(F32)
-    data_ref[4:5, :] = value_ref[...]
-    data_ref[5:6, :] = var_ref[...]
-    data_ref[8:72, :] = noise_ref[...]
-    n_obs = batch_ref.shape[1]
+    data_ref[3:4, :] = ints_ref[...].astype(F32)
+    data_ref[4:5, :] = floats_ref[0]
+    data_ref[5:6, :] = floats_ref[1]
+    data_ref[6:8, :] = jnp.zeros((2, n_obs), F32)
+    data_ref[72:128, :] = jnp.zeros((56, n_obs), F32)
     square = (n_obs, n_obs)
     at_row, at_lane = lax.broadcasted_iota(jnp.int32, square, 0), lax.broadcasted_iota(jnp.int32, square, 1)
     before = (at_row < at_lane).astype(F32).astype(BF16)
@@ -309,30 +311,109 @@
     chosen = (at_row.astype(F32) == rank).astype(F32).astype(BF16)
     data = data_ref[...]
     high = data.astype(BF16)
-    rest = data - high.astype(F32)
-    middle, low = split(rest)
+    middle, low = split(data - high.astype(F32))
     thirds = dot_nt(chosen, jnp.concatenate([high, middle, low], axis=0))
     table = (thirds[:, 0:128] + thirds[:, 128:256]) + thirds[:, 256:384]
     cols_ref[...] = table[:, 0:8]
     rows_ref[...] = table.T[0:72]
+
+    load_tile.wait()
+    for x in range(rows_x):
+        first_ref[x : x + 1, :] = ens_ref[x, 0:1, :]
+        last_ref[x : x + 1, :] = ens_ref[x, rows_y - 1 : rows_y, :]
+
+    pl.semaphore_wait(barrier, n_x + n_y - 2)
+
+    def halo(slot, src, dst, axis, target):
+        return pltpu.make_async_remote_copy(
+            src_ref=src, dst_ref=dst, send_sem=halo_send.at[slot], recv_sem=halo_recv.at[slot],
+            device_id={axis: target}, device_id_type=MESH,
+        )
+
+    copies = (
+        (halo(0, ens_ref.at[rows_x - 1], west_ref, "gx", lax.rem(gx + 1, n_x)), gx < n_x - 1, gx > 0, west_ref),
+        (halo(1, ens_ref.at[0], east_ref, "gx", lax.rem(gx + n_x - 1, n_x)), gx > 0, gx < n_x - 1, east_ref),
+        (halo(2, last_ref, south_ref, "gy", lax.rem(gy + 1, n_y)), gy < n_y - 1, gy > 0, south_ref),
+        (halo(3, first_ref, north_ref, "gy", lax.rem(gy + n_y - 1, n_y)), gy > 0, gy < n_y - 1, north_ref),
+    )
+    for copy, sends, _, _ in copies:
+        pl.when(sends)(copy.start)
+
+    load_weights.wait()
+    for y in range(rows_y):
+        merged = jnp.zeros((rows_x, 128), F32)
+        group = lax.broadcasted_iota(jnp.int32, (rows_x, 128), 1) // LEV
+        for k in range(4):
+            block = w_ref[k, :, 128 * (y // 4) : 128 * (y // 4) + 128]
+            low_lanes = pltpu.roll(block, 128 - 32 * (y % 4), 1) if y % 4 else block
+            spread_ref[pl.ds(k * cells + y, rows_x, stride=rows_y), :] = low_lanes
+            turn = (32 * k - 32 * (y % 4)) % 128
+            merged = jnp.where(group == k, pltpu.roll(block, turn, 1) if turn else block, merged)
+        point_ref[pl.ds(y, rows_x, stride=rows_y), :] = merged
+
     obs_x = table[:, 0:1] - (gx * rows_x).astype(F32)
     obs_y = table[:, 1:2] - (gy * rows_y).astype(F32)
+    obs_l = table[:, 2:3]
     inside = (obs_x >= 0.0) & (obs_x < rows_x) & (obs_y >= 0.0) & (obs_y < rows_y)
-    place = jnp.where(inside, obs_x * rows_y + obs_y, -1.0)
-    pick_ref[...] = (
-        lax.broadcasted_iota(jnp.int32, pick_ref.shape, 1).astype(F32) == place
-    ).astype(F32).astype(BF16)
-    obs_l = table[:, 2:3]
+
+    def place(value):
+        return jnp.where(inside, value, -1.0)
+
+    centre = obs_x * rows_y + obs_y
+    at_west = place(jnp.where(obs_x > 0.0, centre - rows_y, cells + obs_y))
+    at_east = place(jnp.where(obs_x < rows_x - 1.0, centre + rows_y, cells + rows_y + obs_y))
+    at_south = place(jnp.where(obs_y > 0.0, centre - 1.0, cells + 2 * rows_y + obs_x))
+    at_north = place(jnp.where(obs_y < rows_y - 1.0, centre + 1.0, cells + 2 * rows_y + rows_x + obs_x))
+    centre = place(centre)
+    lane = lax.broadcasted_iota(jnp.int32, (n_obs, 256), 1).astype(F32)
+    is_centre = lane == centre
+    high, low = split(point_ref[...])
+    both = dot(
+        is_centre.astype(F32).astype(BF16)[:, 0:cells], jnp.concatenate([high, low], axis=1)
+    )
+    mine = both[:, 0:128] + both[:, 128:256]
+    lane_level = lax.broadcasted_iota(jnp.int32, (n_obs, 128), 1) % LEV
+    mine = jnp.where(lane_level.astype(F32) == obs_l, mine, 0.0)
+    high, low = split(mine)
+    group = lax.broadcasted_iota(jnp.int32, (128, 512), 0) // LEV == lax.broadcasted_iota(jnp.int32, (128, 512), 1) // 128
+    group = group.astype(F32).astype(BF16)
+    coeffs = dot(jnp.concatenate([high, low], axis=1), jnp.concatenate([group, group], axis=0))
+    coeffs = [jnp.concatenate([coeffs[:, 128 * k : 128 * k + 128]] * 2, axis=1) for k in range(4)]
+    mix = jnp.where(is_centre, 1.0 - ((coeffs[0] + coeffs[1]) + (coeffs[2] + coeffs[3])), 0.0)
+    for k, at in enumerate((at_west, at_east, at_south, at_north)):
+        mix = jnp.where(lane == at, coeffs[k], mix)
+    high, low = split(mix)
+    mix_ref[:, 0:256] = high
+    mix_ref[:, 256:512] = low
+    edge_ref[:, 0:64] = high[:, 192:256]
+    edge_ref[:, 64:128] = low[:, 192:256]
+    edge_ref[:, 128:192] = high[:, 192:256]
     pair = jnp.floor(obs_l * 0.5)
     odd = obs_l - 2.0 * pair
-
-    for k in range(4):
-        for y in range(rows_y):
-            block = w_ref[k, :, 128 * (y // 4) : 128 * (y // 4) + 128]
-            if y % 4:
-                block = pltpu.roll(block, 128 - 32 * (y % 4), 1)
-            spread_ref[pl.ds(k * cells + y, rows_x, stride=rows_y), :] = block
     found_ref[...] = jnp.zeros(found_ref.shape, F32)
+
+    def take(step, here):
+        found = found_ref[...]
+        for h in range(2):
+            found = jnp.where(
+                pair == (2 * step + h).astype(F32), found + here[:, h * 128 : h * 128 + 128], found
+            )
+        found_ref[...] = found
+
+    def lanes_of(step):
+        return pl.ds(pl.multiple_of(step * 256, 256), 256)
+
+    def own_cells(step, carry):
+        high, low = split(ens_ref[:, :, lanes_of(step)].reshape(cells, 256))
+        take(
+            step,
+            dot(mix_ref[:, 0:cells], high)
+            + dot(mix_ref[:, 256 : 256 + cells], high)
+            + dot(mix_ref[:, 0:cells], low),
+        )
+        return carry
+
+    lax.fori_loop(0, 8, own_cells, 0)
 
     for copy, _, receives, halo_ref in copies:
         pl.when(receives)(copy.wait_recv)
@@ -341,15 +422,24 @@
         def _():
             halo_ref[...] = jnp.zeros(halo_ref.shape, F32)
 
+    def cells_beside(step, carry):
+        lanes = lanes_of(step)
+        high, low = split(
+            jnp.concatenate([west_ref[:, lanes], east_ref[:, lanes], south_ref[:, lanes], north_ref[:, lanes]], axis=0)
+        )
+        take(step, dot(edge_ref[...], jnp.concatenate([high, high, low], axis=0)))
+        return carry
+
+    lax.fori_loop(0, 8, cells_beside, 0)
+
     def forecast_step(step, carry):
-        lanes = pl.ds(pl.multiple_of(step * 256, 256), 256)
+        lanes = lanes_of(step)
         level = lax.broadcasted_iota(jnp.int32, (128, 256), 0)
         column = lax.broadcasted_iota(jnp.int32, (128, 256), 1) // 64 + 4 * step
         ones = (level == column).astype(F32).astype(BF16)
         high, low = split(spread_ref[...])
         weights = dot(jnp.concatenate([high, low], axis=1), jnp.concatenate([ones, ones], axis=0))
         side = lax.broadcasted_iota(jnp.int32, (rows_y, 256), 0)
-        parts = []
         for x in range(rows_x):
             q = ens_ref[x, :, lanes]
             west = west_ref[:, lanes] if x == 0 else ens_ref[x - 1, :, lanes]
@@ -360,27 +450,16 @@
             for k, other in enumerate((west, east, south, north)):
                 at = k * cells + x * rows_y
                 total = total + weights[at : at + rows_y] * (other - q)
-            parts.append(total)
-        step_rows = jnp.concatenate(parts, axis=0)
-        f_ref[:, lanes] = step_rows
-        high, low = split(step_rows)
-        here = dot(pick_ref[:, 0:cells], high) + dot(pick_ref[:, 0:cells], low)
-        found = found_ref[...]
-        for h in range(2):
-            found = found + jnp.where(
-                pair == (2 * step + h).astype(F32), here[:, h * 128 : h * 128 + 128], 0.0
-            )
-        found_ref[...] = found
+            f_ref[x * rows_y : x * rows_y + rows_y, lanes] = total
         return carry
 
-    lax.fori_loop(0, 8, forecast_step, 0)
     found = found_ref[...]
     turned = pltpu.roll(found, 64, 1)
     left = jnp.where(odd == 0.0, found, turned)
     right = jnp.where(odd == 0.0, turned, found)
     half = n_obs // 2
-    lane = lax.broadcasted_iota(jnp.int32, (half, 128), 1)
-    part_ref[...] = jnp.where(lane < 64, left[:half], right[half:])
+    side = lax.broadcasted_iota(jnp.int32, (half, 128), 1)
+    part_ref[...] = jnp.where(side < 64, left[:half], right[half:])
 
     share = half // n_y
 
@@ -399,6 +478,7 @@
     ]
     for copy in first:
         copy.start()
+    lax.fori_loop(0, 3, forecast_step, 0)
     total = part_ref[rows_of(gy), :]
     for s, copy in enumerate(first, 1):
         copy.wait_recv()
@@ -407,6 +487,7 @@
     second = [send(s, "gx", gx, n_x, sum_ref, got_x_ref.at[s], send_2, recv_2) for s in range(1, n_x)]
     for copy in second:
         copy.start()
+    lax.fori_loop(3, 6, forecast_step, 0)
     for s, copy in enumerate(second, 1):
         copy.wait_recv()
         total = total + got_x_ref[s]
@@ -417,6 +498,7 @@
     for copy in third:
         copy.start()
     all_ref[rows_of(gy), :] = total
+    lax.fori_loop(6, 8, forecast_step, 0)
     for copy, sends, _, _ in copies:
         pl.when(sends)(copy.wait_send)
     for copy in first + second:
@@ -443,9 +525,15 @@
             jax.ShapeDtypeStruct((72, n_obs), F32),
             jax.ShapeDtypeStruct((n_obs, 8), F32),
         ),
-        in_specs=[vmem] * 8,
+        in_specs=[pl.BlockSpec(memory_space=pltpu.HBM)] * 8,
         out_specs=(vmem,) * 4,
         scratch_shapes=[
+            pltpu.VMEM(ensemble.shape, F32),
+            pltpu.VMEM(weights.shape, F32),
+            pltpu.VMEM(obs_cell.shape, jnp.int32),
+            pltpu.VMEM((1, n_obs), jnp.int32),
+            pltpu.VMEM((1, n_obs), jnp.int32),
+            pltpu.VMEM((2, 1, n_obs), F32),
             pltpu.VMEM((rows_y, width), F32),
             pltpu.VMEM((rows_y, width), F32),
             pltpu.VMEM((rows_x, width), F32),
@@ -454,7 +542,9 @@
             pltpu.VMEM((rows_x, width), F32),
             pltpu.VMEM((128, n_obs), F32),
             pltpu.VMEM((4 * cells, 128), F32),
-            pltpu.VMEM((n_obs, 256), BF16),
+            pltpu.VMEM((cells, 128), F32),
+            pltpu.VMEM((n_obs, 512), BF16),
+            pltpu.VMEM((n_obs, 192), BF16),
             pltpu.VMEM((n_obs, 128), F32),
             pltpu.VMEM((n_obs // 2, 128), F32),
             pltpu.VMEM((n_y, share, 128), F32),
@@ -462,7 +552,7 @@
             pltpu.VMEM((n_x, share, 128), F32),
             pltpu.VMEM((share, 128), F32),
             pltpu.VMEM((n_obs // 2, 128), F32),
-            dma((4,)), dma((4,)),
+            dma((8,)), dma((4,)), dma((4,)),
             dma((n_y,)), dma((n_y,)), dma((n_x,)), dma((n_x,)), dma((n_y,)), dma((n_y,)),
         ],
         compiler_params=pltpu.CompilerParams(
@@ -470,8 +560,13 @@
         ),
         name="forecast_and_gather",
     )(
-        ensemble, weights, obs_cell, obs_batch.reshape(1, n_obs), obs_radius.reshape(1, n_obs),
-        obs_value.reshape(1, n_obs), obs_var.reshape(1, n_obs), obs_noise,
+        *(
+            pltpu.with_memory_space_constraint(value, pltpu.HBM)
+            for value in (
+                ensemble, weights, obs_cell, obs_batch.reshape(1, n_obs), obs_radius.reshape(1, n_obs),
+                obs_value.reshape(1, n_obs), obs_var.reshape(1, n_obs), obs_noise,
+            )
+        )
     )
 
 

time: 70.8 us -> 60.1 us (0.85)
  local copies, waits for them, and re-layouts: 6.62 us -> 0 us
  Pallas kernels: 63.8 us -> 60 us
    unnamed x16 -> x0, local copies, waits for them, and re-layouts: 6.62 us -> none
    pallas_call x1, Pallas kernels: 37.9 us -> 34 us  [forecast_and_gather(): pl.pallas_call(functools.partial(forecast_kernel, n_x, n_y), out_shape=(j...]
where the time goes in v2:
time: 60.1 us; the launch traced here: 60 us
  Pallas kernels  60 us (100%)
    pallas_call x1, Pallas kernels, forecast_and_gather(): pl.pallas_call(functools.partial(forecast_kernel, n_x, n_y), out_shape=(j...  34 us
    pallas_call x1, Pallas kernels, analyse(): pl.pallas_call(functools.partial(analysis_kernel, axes), out_shape=jax.Sh...  26 us

profile of v2, /device:TPU:1, one launch (start us, length us, event | category | flops | bytes accessed | tf_op | source)
XLA Modules:
  0.0 60.0 jit_solution(12918505901910866908)
XLA Ops:
  0.0 34.0 %forecast_and_gather.1 = (f32[192,2048]{1,0:T(8,128)S(1)}, f32[256,128]{1,0:T(8,128)S(1)}, f32[72,512]{1,0:T(8,128)S(1)}, f32[512,8]{1,0:T(8,128)S(1)}) custom-call(f32[8,24,2048]{2,1,0:T(8,128)} %ens_hbm.1, f32[4,8,768]{2,1,0:T(8,128)} %w_hbm.1, s32[3,512]{1,0:T(4,128)} %cell_hbm.1, s32[1,512]{1,0:T(1,128)} %bitcast.5, s32[1,512]{1,0:T(1,128)} %bitcast.6, ...), custom_call_target="tpu_custom_call" | custom-call | tf_op jit(solution)/shard_map/forecast_and_gather/pallas_call | solution.py:520
  34.0 26.0 %analysis.1 = f32[192,2048]{1,0:T(8,128)} custom-call(f32[192,2048]{1,0:T(8,128)S(1)} %get-tuple-element.9.f_ref, f32[256,128]{1,0:T(8,128)S(1)} %get-tuple-element.10.p_ref, f32[72,512]{1,0:T(8,128)S(1)} %get-tuple-element.11.rows_ref, f32[512,8]{1,0:T(8,128)S(1)} %get-tuple-element.12.cols_ref), custom_call_target="tpu_custom_call" | custom-call | tf_op jit(solution)/shard_map/analysis/pallas_call | solution.py:231

commit v3 on v2

--- a/solution.py
+++ b/solution.py
@@ -9,6 +9,7 @@
 MEM = 64
 LEV = 32
 OBS_B = 128
+HALF = 64
 NBATCH = 4
 HIGHEST = lax.Precision.HIGHEST
 F32 = jnp.float32
@@ -30,60 +31,74 @@
     return high, (value - high.astype(F32)).astype(BF16)
 
 
-def eliminate_four(rows, first):
+def invert_two(a, b, d):
+    inv = 1.0 / (a * d - b * b)
+    return d * inv, -b * inv, a * inv
+
+
+def invert_four(m):
+    p00, p01, p11 = invert_two(m[0][0], m[1][0], m[1][1])
+    x20, x21 = m[2][0] * p00 + m[2][1] * p01, m[2][0] * p01 + m[2][1] * p11
+    x30, x31 = m[3][0] * p00 + m[3][1] * p01, m[3][0] * p01 + m[3][1] * p11
+    s22 = m[2][2] - (x20 * m[2][0] + x21 * m[2][1])
+    s32 = m[3][2] - (x30 * m[2][0] + x31 * m[2][1])
+    s33 = m[3][3] - (x30 * m[3][0] + x31 * m[3][1])
+    q22, q32, q33 = invert_two(s22, s32, s33)
+    y20, y21 = q22 * x20 + q32 * x30, q22 * x21 + q32 * x31
+    y30, y31 = q32 * x20 + q33 * x30, q32 * x21 + q33 * x31
+    low = [
+        [p00 + (x20 * y20 + x30 * y30)],
+        [p01 + (x20 * y21 + x30 * y31), p11 + (x21 * y21 + x31 * y31)],
+        [-y20, -y21, q22],
+        [-y30, -y31, q32, q33],
+    ]
+    return [[low[max(i, j)][min(i, j)] for j in range(4)] for i in range(4)]
+
+
+def total(terms):
+    terms = list(terms)
+    while len(terms) > 1:
+        terms = [sum(terms[i + 1 : i + 2], terms[i]) for i in range(0, len(terms), 2)]
+    return terms[0]
+
+
+def eliminate_eight(rows):
     blocks = len(rows)
     shape = (8, 128)
+    four = range(4)
     columns = [
-        [jnp.broadcast_to(rows[v][0][:, first + j : first + j + 1], shape) for v in range(blocks)]
-        for j in range(4)
+        [jnp.broadcast_to(rows[v][0][:, j : j + 1], shape) for v in range(blocks)] for j in range(8)
     ]
 
     def entry(i, j):
-        return jnp.broadcast_to(columns[j][0][first + i : first + i + 1, :], shape)
-
-    a00, a01, a11 = entry(0, 0), entry(0, 1), entry(1, 1)
-    a20, a21, a30, a31 = entry(2, 0), entry(2, 1), entry(3, 0), entry(3, 1)
-    a22, a32, a33 = entry(2, 2), entry(3, 2), entry(3, 3)
-    inv = 1.0 / (a00 * a11 - a01 * a01)
-    p00, p01, p11 = a11 * inv, -a01 * inv, a00 * inv
-    x20, x21 = a20 * p00 + a21 * p01, a20 * p01 + a21 * p11
-    x30, x31 = a30 * p00 + a31 * p01, a30 * p01 + a31 * p11
-    s22 = a22 - (x20 * a20 + x21 * a21)
-    s32 = a32 - (x30 * a20 + x31 * a21)
-    s33 = a33 - (x30 * a30 + x31 * a31)
-    inv = 1.0 / (s22 * s33 - s32 * s32)
-    q22, q32, q33 = s33 * inv, -s32 * inv, s22 * inv
-    lane_row = lax.broadcasted_iota(jnp.int32, shape, 0)
+        return jnp.broadcast_to(columns[j][0][i : i + 1, :], shape)
+
+    first = [[entry(i, j) for j in range(i + 1)] for i in four]
+    cross = [[entry(4 + i, j) for j in four] for i in four]
+    second = [[entry(4 + i, 4 + j) for j in range(i + 1)] for i in four]
+    p = invert_four(first)
+    x = [[total(cross[i][k] * p[k][j] for k in four) for j in four] for i in four]
+    q = invert_four(
+        [[second[i][j] - total(x[i][k] * cross[j][k] for k in four) for j in range(i + 1)] for i in four]
+    )
+    at = lax.broadcasted_iota(jnp.int32, shape, 0)
     result = [[None] * len(rows[0]) for _ in range(blocks)]
     for col in range(len(rows[0])):
-        r0, r1, r2, r3 = (
-            jnp.broadcast_to(rows[0][col][first + i : first + i + 1, :], shape) for i in range(4)
-        )
-        t2 = r2 - (x20 * r0 + x21 * r1)
-        t3 = r3 - (x30 * r0 + x31 * r1)
-        n2 = q22 * t2 + q32 * t3
-        n3 = q32 * t2 + q33 * t3
-        n0 = p00 * r0 + p01 * r1 - (x20 * n2 + x30 * n3)
-        n1 = p01 * r0 + p11 * r1 - (x21 * n2 + x31 * n3)
-        for v in range(blocks):
-            value = rows[v][col] - (
-                (columns[0][v] * n0 + columns[1][v] * n1)
-                + (columns[2][v] * n2 + columns[3][v] * n3)
-            )
-            if v == 0:
-                value = jnp.where(lane_row == first, n0, value)
-                value = jnp.where(lane_row == first + 1, n1, value)
-                value = jnp.where(lane_row == first + 2, n2, value)
-                value = jnp.where(lane_row == first + 3, n3, value)
-            result[v][col] = value
-    return result
-
-
-def eliminate_eight(rows):
-    rows = eliminate_four(rows, 0)
-    rows = eliminate_four(rows, 4)
-    rows = [[pltpu.roll(row[0], 120, 1)] + row[1:] for row in rows]
-    return rows[1:] + rows[:1]
+        r = [jnp.broadcast_to(rows[0][col][i : i + 1, :], shape) for i in range(8)]
+        t = [r[4 + i] - total(x[i][k] * r[k] for k in four) for i in four]
+        upper = [total(q[i][k] * t[k] for k in four) for i in four]
+        lower = [
+            total(p[i][k] * r[k] for k in four) - total(x[k][i] * upper[k] for k in four) for i in four
+        ]
+        solved = lower + upper
+        for v in range(1, blocks):
+            result[v][col] = rows[v][col] - total(columns[k][v] * solved[k] for k in range(8))
+        value = solved[0]
+        for k in range(1, 8):
+            value = jnp.where(at == k, solved[k], value)
+        result[0][col] = value
+    result = [[pltpu.roll(row[0], 120, 1)] + row[1:] for row in result]
+    return result[1:] + result[:1]
 
 
 def flat(rows):
@@ -100,7 +115,8 @@
 
 
 def analysis_kernel(
-    axes, f_ref, p_ref, rows_ref, cols_ref, o_ref, state_ref, near_ref, w1_ref, w2_ref, hor_ref, ver_ref
+    axes, f_ref, p_ref, rows_ref, cols_ref, select_ref, across_ref, down_ref, most_ref,
+    o_ref, state_ref, near_ref, w1_ref, w2_ref, hor_ref, ver_ref,
 ):
     cells = f_ref.shape[0]
     start_x, start_y = axes()
@@ -128,10 +144,7 @@
         system = product[:64] + eye.astype(F32)
         rhs = scaled * inv_dev
         rows = [[system[8 * v : 8 * v + 8], rhs[8 * v : 8 * v + 8]] for v in range(8)]
-        return anomaly, innovation * variance_inverse(inv_dev), product[64:, :64], rows
-
-    def variance_inverse(inv_dev):
-        return inv_dev * inv_dev
+        return anomaly, innovation * (inv_dev * inv_dev), product[64:, :64], rows
 
     def near(batch, anomaly):
         low, high = batch * OBS_B, (batch + 1) * OBS_B
@@ -149,26 +162,21 @@
             at = (later - batch - 1) * OBS_B
             near_ref[:, at : at + OBS_B] = links[:, at : at + OBS_B] * (across / (down * (MEM - 1)))
 
-    def tile_begin(batch, anomaly, gain):
-        zero = jnp.zeros((64, 128), BF16)
+    def twice(value):
+        zero = jnp.zeros(value.shape, value.dtype)
+        return jnp.concatenate(
+            [jnp.concatenate([value, zero], axis=1), jnp.concatenate([zero, value], axis=1)], axis=0
+        )
+
+    def all_begin(batch, anomaly, gain):
         high, low = split(anomaly)
-        high_two = jnp.concatenate(
-            [jnp.concatenate([high, zero], axis=1), jnp.concatenate([zero, high], axis=1)], axis=0
-        )
+        high_two = twice(high)
         w1_ref[0:128, :] = high_two
         w1_ref[128:256, :] = high_two
-        w1_ref[256:384, :] = jnp.concatenate(
-            [jnp.concatenate([low, zero], axis=1), jnp.concatenate([zero, low], axis=1)], axis=0
-        )
-        turned = gain.T
-        high, low = split(turned)
-        zero = jnp.zeros((128, 64), BF16)
-        w2_ref[:, 0:128] = jnp.concatenate(
-            [jnp.concatenate([high, zero], axis=1), jnp.concatenate([zero, high], axis=1)], axis=0
-        )
-        w2_ref[:, 128:256] = jnp.concatenate(
-            [jnp.concatenate([low, zero], axis=1), jnp.concatenate([zero, low], axis=1)], axis=0
-        )
+        w1_ref[256:384, :] = twice(low)
+        high, low = split(gain.T)
+        w2_ref[:, 0:128] = twice(high)
+        w2_ref[:, 128:256] = twice(low)
         cell = lax.broadcasted_iota(jnp.int32, (cells, 1), 0)
         level = lax.broadcasted_iota(jnp.int32, (LEV, 1), 0).astype(F32)
         cell_x = (cell // 24 + start_x).astype(F32)
@@ -179,8 +187,29 @@
         hor_ref[...] = across
         ver_ref[...] = 1.0 / (down * (MEM - 1))
 
-    def tile_step(src_ref, step):
-        lanes = [pl.ds(pl.multiple_of(step * 256 + 128 * h, 128), 128) for h in range(2)]
+    def some_begin(batch, anomaly, gain):
+        chosen = select_ref[batch * OBS_B : (batch + 1) * OBS_B, :]
+        kept = dot_nt(jnp.concatenate(split(anomaly), axis=0), chosen)
+        first = lax.broadcasted_iota(jnp.int32, (MEM, 128), 1) < HALF
+        high, low = kept[:MEM], kept[MEM:]
+        upper = jnp.concatenate([jnp.where(first, high, 0.0), jnp.where(first, low, 0.0)], axis=1)
+        lower = jnp.concatenate([jnp.where(first, 0.0, high), jnp.where(first, 0.0, low)], axis=1)
+        both = jnp.concatenate([upper, lower], axis=0).astype(BF16)
+        w1_ref[0:128, :] = both
+        w1_ref[128:256, :] = both
+        high, low = split(gain)
+        kept = dot_nt(chosen, jnp.concatenate([high, high, low, low], axis=0))
+        slot = lax.broadcasted_iota(jnp.int32, (128, 256), 0) // HALF
+        member = (lax.broadcasted_iota(jnp.int32, (128, 256), 1) // MEM) % 2
+        both = jnp.where(slot == member, kept, 0.0).astype(BF16)
+        w2_ref[0:128, :] = both
+        w2_ref[128:256, :] = both
+
+    def lanes_of(step):
+        return [pl.ds(pl.multiple_of(step * 256 + 128 * h, 128), 128) for h in range(2)]
+
+    def all_step(batch, src_ref, step):
+        lanes = lanes_of(step)
         state = jnp.concatenate([src_ref[:, lanes[0]], src_ref[:, lanes[1]]], axis=0)
         high, low = split(state)
         link = dot(jnp.concatenate([high, low], axis=1), w1_ref[0:256, :]) + dot(high, w1_ref[256:384, :])
@@ -199,39 +228,66 @@
         for h in range(2):
             o_ref[:, lanes[h]] = state[h * cells : (h + 1) * cells]
 
-    for batch in range(NBATCH + 1):
-        if batch < NBATCH:
-            anomaly, direct, cross, rows = solve_begin(batch)
-            near(batch, anomaly)
-            values = flat(rows)
-        else:
-            values = ()
-
-        def step_body(step, values):
-            if batch > 0:
-                tile_step(f_ref if batch == 1 else o_ref, step)
+    def some_step(batch, src_ref, step):
+        lanes = lanes_of(step)
+        state = jnp.concatenate([src_ref[:, lanes[0]], src_ref[:, lanes[1]]], axis=0)
+        link = dot(jnp.concatenate(split(state), axis=1), w1_ref[0:256, :])
+        parts = []
+        for h in range(2):
+            rows = slice(h * cells, (h + 1) * cells)
+            down = down_ref[pl.ds(16 * batch + 2 * step + h, 1), :]
+            across = across_ref[batch * cells : (batch + 1) * cells, :]
+            parts.append((link[rows, :128] + link[rows, 128:]) * (across * down))
+        wide = dot(jnp.concatenate(split(jnp.concatenate(parts, axis=0)), axis=1), w2_ref[...])
+        state = state + (wide[:, :128] + wide[:, 128:])
+        for h in range(2):
+            o_ref[:, lanes[h]] = state[h * cells : (h + 1) * cells]
+
+    def process(begin, tile_step):
+        anomaly = None
+        for batch in range(NBATCH + 1):
             if batch < NBATCH:
-                values = flat(eliminate_eight(nested(values, 2)))
-            return values
-
-        values = lax.fori_loop(0, 8, step_body, values)
-        if batch < NBATCH:
-            solved = jnp.concatenate([row[1] for row in nested(values, 2)], axis=0)
-            gain = direct - dot(cross, solved, HIGHEST)
-            if batch < NBATCH - 1:
-                high = (batch + 1) * OBS_B
-                state_ref[:, high:] = state_ref[:, high:] + dot(
-                    gain, near_ref[:, : NBATCH * OBS_B - high], HIGHEST
-                )
-            tile_begin(batch, anomaly, gain)
-
-
-def analyse(axes, forecast, packed, rows, cols):
+                anomaly, direct, cross, rows = solve_begin(batch)
+                near(batch, anomaly)
+                values = flat(rows)
+            else:
+                values = ()
+
+            def step_body(step, values):
+                if batch > 0:
+                    tile_step(batch - 1, f_ref if batch == 1 else o_ref, step)
+                if batch < NBATCH:
+                    values = flat(eliminate_eight(nested(values, 2)))
+                return values
+
+            values = lax.fori_loop(0, 8, step_body, values)
+            if batch < NBATCH:
+                solved = jnp.concatenate([row[1] for row in nested(values, 2)], axis=0)
+                gain = direct - dot(cross, solved, HIGHEST)
+                if batch < NBATCH - 1:
+                    high = (batch + 1) * OBS_B
+                    state_ref[:, high:] = state_ref[:, high:] + dot(
+                        gain, near_ref[:, : NBATCH * OBS_B - high], HIGHEST
+                    )
+                begin(batch, anomaly, gain)
+
+    fits = jnp.max(most_ref[...]) <= HALF
+
+    @pl.when(fits)
+    def _():
+        process(some_begin, some_step)
+
+    @pl.when(jnp.logical_not(fits))
+    def _():
+        process(all_begin, all_step)
+
+
+def analyse(axes, forecast, *rest):
     cells = forecast.shape[0]
     return pl.pallas_call(
         functools.partial(analysis_kernel, axes),
         out_shape=jax.ShapeDtypeStruct(forecast.shape, F32),
-        in_specs=[pl.BlockSpec(memory_space=pltpu.VMEM)] * 4,
+        in_specs=[pl.BlockSpec(memory_space=pltpu.VMEM)] * 8,
         out_specs=pl.BlockSpec(memory_space=pltpu.VMEM),
         scratch_shapes=[
             pltpu.VMEM((MEM, NBATCH * OBS_B), F32),
@@ -243,16 +299,51 @@
         ],
         compiler_params=pltpu.CompilerParams(vmem_limit_bytes=48 * 1024 * 1024),
         name="analysis",
-    )(forecast, packed, rows, cols)
+    )(forecast, *rest)
 
 
 MESH = pl.DeviceIdType.MESH
+
+
+def tables(start_x, start_y, rows_ref, select_ref, across_ref, down_ref, most_ref):
+    cells = across_ref.shape[0] // NBATCH
+    most = jnp.zeros((8, 128), F32)
+    square = (128, 128)
+    before = (
+        lax.broadcasted_iota(jnp.int32, square, 0) < lax.broadcasted_iota(jnp.int32, square, 1)
+    ).astype(F32).astype(BF16)
+    slot = (lax.broadcasted_iota(jnp.int32, square, 0) % HALF).astype(F32)
+    cell = lax.broadcasted_iota(jnp.int32, (cells, 128), 0)
+    cell_x, cell_y = (cell // 24).astype(F32), (cell % 24).astype(F32)
+    level = 2 * lax.broadcasted_iota(jnp.int32, (LEV // 2, 128), 0)
+    level = (level + lax.broadcasted_iota(jnp.int32, (LEV // 2, 128), 1) // HALF).astype(F32)
+    kind = lax.broadcasted_iota(jnp.int32, (8, 128), 0)
+    for batch in range(NBATCH):
+        low = batch * OBS_B
+        x, y, l, r = (rows_ref[i : i + 1, low : low + OBS_B] for i in range(4))
+        x, y = x - start_x.astype(F32), y - start_y.astype(F32)
+        dx = jnp.maximum(jnp.maximum(-x, x - 7.0), 0.0)
+        dy = jnp.maximum(jnp.maximum(-y, y - 23.0), 0.0)
+        reaches = dx * dx + dy * dy < r * r
+        flags = jnp.broadcast_to(reaches.astype(F32), (8, 128))
+        position = dot(flags.astype(BF16), before)[0:1]
+        most = jnp.maximum(most, jnp.sum(flags, axis=1, keepdims=True))
+        chosen = jnp.where((slot == position) & reaches, 1.0, 0.0).astype(BF16)
+        select_ref[low : low + OBS_B, :] = chosen
+        facts = jnp.where(kind == 0, x, jnp.where(kind == 1, y, jnp.where(kind == 2, l, jnp.where(kind == 3, r, 1.0))))
+        kept = dot_nt(facts.astype(BF16), chosen)
+        across, down = taper_of(
+            cell_x - kept[0:1], cell_y - kept[1:2], level - kept[2:3], kept[3:4] + (1.0 - kept[4:5])
+        )
+        across_ref[batch * cells : (batch + 1) * cells, :] = across
+        down_ref[batch * LEV // 2 : (batch + 1) * LEV // 2, :] = 1.0 / (down * (MEM - 1))
+    most_ref[...] = most
 
 
 def forecast_kernel(
     n_x, n_y,
     ens_hbm, w_hbm, cell_hbm, batch_hbm, radius_hbm, value_hbm, var_hbm, noise_hbm,
-    f_ref, p_ref, rows_ref, cols_ref,
+    f_ref, p_ref, rows_ref, cols_ref, select_ref, across_ref, down_ref, most_ref,
     ens_ref, w_ref, cell_ref, batch_ref, ints_ref, floats_ref,
     west_ref, east_ref, south_ref, north_ref, first_ref, last_ref,
     data_ref, spread_ref, point_ref, mix_ref, edge_ref, found_ref,
@@ -478,7 +569,8 @@
     ]
     for copy in first:
         copy.start()
-    lax.fori_loop(0, 3, forecast_step, 0)
+    tables(gx * rows_x, gy * rows_y, rows_ref, select_ref, across_ref, down_ref, most_ref)
+    lax.fori_loop(0, 2, forecast_step, 0)
     total = part_ref[rows_of(gy), :]
     for s, copy in enumerate(first, 1):
         copy.wait_recv()
@@ -487,7 +579,7 @@
     second = [send(s, "gx", gx, n_x, sum_ref, got_x_ref.at[s], send_2, recv_2) for s in range(1, n_x)]
     for copy in second:
         copy.start()
-    lax.fori_loop(3, 6, forecast_step, 0)
+    lax.fori_loop(2, 5, forecast_step, 0)
     for s, copy in enumerate(second, 1):
         copy.wait_recv()
         total = total + got_x_ref[s]
@@ -498,7 +590,7 @@
     for copy in third:
         copy.start()
     all_ref[rows_of(gy), :] = total
-    lax.fori_loop(6, 8, forecast_step, 0)
+    lax.fori_loop(5, 8, forecast_step, 0)
     for copy, sends, _, _ in copies:
         pl.when(sends)(copy.wait_send)
     for copy in first + second:
@@ -524,9 +616,13 @@
             jax.ShapeDtypeStruct((n_obs // 2, 128), F32),
             jax.ShapeDtypeStruct((72, n_obs), F32),
             jax.ShapeDtypeStruct((n_obs, 8), F32),
+            jax.ShapeDtypeStruct((n_obs, 128), BF16),
+            jax.ShapeDtypeStruct((NBATCH * cells, 128), F32),
+            jax.ShapeDtypeStruct((NBATCH * LEV // 2, 128), F32),
+            jax.ShapeDtypeStruct((8, 128), F32),
         ),
         in_specs=[pl.BlockSpec(memory_space=pltpu.HBM)] * 8,
-        out_specs=(vmem,) * 4,
+        out_specs=(vmem,) * 8,
         scratch_shapes=[
             pltpu.VMEM(ensemble.shape, F32),
             pltpu.VMEM(weights.shape, F32),
@@ -575,9 +671,9 @@
 
     def body(ensemble, *rest):
         rows_x, rows_y, width = ensemble.shape
-        forecast, packed, rows, cols = forecast_and_gather(n_x, n_y, ensemble, *rest)
+        found = forecast_and_gather(n_x, n_y, ensemble, *rest)
         analysis = analyse(
-            lambda: (lax.axis_index("gx") * rows_x, lax.axis_index("gy") * rows_y), forecast, packed, rows, cols
+            lambda: (lax.axis_index("gx") * rows_x, lax.axis_index("gy") * rows_y), *found
         )
         return analysis.reshape(rows_x, rows_y, width)
 

time: 60.1 us -> 54.5 us (0.907)
  Pallas kernels: 60 us -> 54.4 us
    pallas_call x1, Pallas kernels: 26 us -> 20.5 us  [analyse(): pl.pallas_call(functools.partial(analysis_kernel, axes), out_shape=jax.Sh...]
where the time goes in v3:
time: 54.5 us; the launch traced here: 54.4 us
  Pallas kernels  54.4 us (100%)
    pallas_call x1, Pallas kernels, forecast_and_gather(): pl.pallas_call(functools.partial(forecast_kernel, n_x, n_y), out_shape=(j...  33.9 us
    pallas_call x1, Pallas kernels, analyse(): pl.pallas_call(functools.partial(analysis_kernel, axes), out_shape=jax.Sh...  20.5 us

profile of v3, /device:TPU:1, one launch (start us, length us, event | category | flops | bytes accessed | tf_op | source)
XLA Modules:
  0.0 54.4 jit_solution(13087546047272748379)
XLA Ops:
  0.0 33.9 %forecast_and_gather.1 = (f32[192,2048]{1,0:T(8,128)S(1)}, f32[256,128]{1,0:T(8,128)S(1)}, f32[72,512]{1,0:T(8,128)S(1)}, f32[512,8]{1,0:T(8,128)S(1)}, bf16[512...) custom-call(f32[8,24,2048]{2,1,0:T(8,128)} %ens_hbm.1, ...), custom_call_target="tpu_custom_call" | custom-call | tf_op jit(solution)/shard_map/forecast_and_gather/pallas_call | solution.py:612
  33.9 20.5 %analysis.1 = f32[192,2048]{1,0:T(8,128)} custom-call(f32[192,2048]{1,0:T(8,128)S(1)} %get-tuple-element.13.f_ref, f32[256,128]{1,0:T(8,128)S(1)} %get-tuple-element.14.p_ref, f32[72,512]{1,0:T(8,128)S(1)} %get-tuple-element.15.rows_ref, f32[512,8]{1,0:T(8,128)S(1)} %get-tuple-element.16.cols_ref, bf16[512,128]{1,0:T(8,128)(2,1)S(1)} %get-tuple-element.17.select_ref, ...), custom_call_target="tpu_custom_call" | custom-call | tf_op jit(solution)/shard_map/analysis/pallas_call | solution.py:287

commit v4 on v3

--- a/solution.py
+++ b/solution.py
@@ -62,12 +62,13 @@
     return terms[0]
 
 
-def eliminate_eight(rows):
-    blocks = len(rows)
+def eliminate_eight(rows, block):
+    low = 8 * block
     shape = (8, 128)
     four = range(4)
     columns = [
-        [jnp.broadcast_to(rows[v][0][:, j : j + 1], shape) for v in range(blocks)] for j in range(8)
+        [jnp.broadcast_to(rows[v][0][:, low + j : low + j + 1], shape) for v in range(block, len(rows))]
+        for j in range(8)
     ]
 
     def entry(i, j):
@@ -82,31 +83,23 @@
         [[second[i][j] - total(x[i][k] * cross[j][k] for k in four) for j in range(i + 1)] for i in four]
     )
     at = lax.broadcasted_iota(jnp.int32, shape, 0)
-    result = [[None] * len(rows[0]) for _ in range(blocks)]
-    for col in range(len(rows[0])):
-        r = [jnp.broadcast_to(rows[0][col][i : i + 1, :], shape) for i in range(8)]
+    result = [list(row) for row in rows]
+    for col in range(2):
+        r = [jnp.broadcast_to(rows[block][col][i : i + 1, :], shape) for i in range(8)]
         t = [r[4 + i] - total(x[i][k] * r[k] for k in four) for i in four]
         upper = [total(q[i][k] * t[k] for k in four) for i in four]
         lower = [
             total(p[i][k] * r[k] for k in four) - total(x[k][i] * upper[k] for k in four) for i in four
         ]
         solved = lower + upper
-        for v in range(1, blocks):
-            result[v][col] = rows[v][col] - total(columns[k][v] * solved[k] for k in range(8))
-        value = solved[0]
-        for k in range(1, 8):
-            value = jnp.where(at == k, solved[k], value)
-        result[0][col] = value
-    result = [[pltpu.roll(row[0], 120, 1)] + row[1:] for row in result]
-    return result[1:] + result[:1]
-
-
-def flat(rows):
-    return tuple(value for row in rows for value in row)
-
-
-def nested(values, width):
-    return [list(values[i : i + width]) for i in range(0, len(values), width)]
+        for v in range(block + 1, len(rows)):
+            result[v][col] = rows[v][col] - total(columns[k][v - block] * solved[k] for k in range(8))
+        if col == 1:
+            value = solved[0]
+            for k in range(1, 8):
+                value = jnp.where(at == k, solved[k], value)
+            result[block][1] = value
+    return result
 
 
 def taper_of(dx, dy, dl, radius):
@@ -138,13 +131,12 @@
         innovation = row_of(4, batch) + deviation * noise - prior
         scaled = anomaly * (inv_dev * (1.0 / (MEM - 1) ** 0.5))
         both = jnp.concatenate([scaled, innovation * inv_dev], axis=0)
-        right = jnp.concatenate([scaled, jnp.zeros((64, OBS_B), F32)], axis=0)
-        product = dot_nt(both, right, HIGHEST)
+        product = dot_nt(scaled, both, HIGHEST)
         eye = lax.broadcasted_iota(jnp.int32, (64, 128), 0) == lax.broadcasted_iota(jnp.int32, (64, 128), 1)
-        system = product[:64] + eye.astype(F32)
+        system = product + eye.astype(F32)
         rhs = scaled * inv_dev
         rows = [[system[8 * v : 8 * v + 8], rhs[8 * v : 8 * v + 8]] for v in range(8)]
-        return anomaly, innovation * (inv_dev * inv_dev), product[64:, :64], rows
+        return anomaly, innovation * (inv_dev * inv_dev), rows
 
     def near(batch, anomaly):
         low, high = batch * OBS_B, (batch + 1) * OBS_B
@@ -206,7 +198,7 @@
         w2_ref[128:256, :] = both
 
     def lanes_of(step):
-        return [pl.ds(pl.multiple_of(step * 256 + 128 * h, 128), 128) for h in range(2)]
+        return [pl.ds(step * 256 + 128 * h, 128) for h in range(2)]
 
     def all_step(batch, src_ref, step):
         lanes = lanes_of(step)
@@ -247,23 +239,17 @@
         anomaly = None
         for batch in range(NBATCH + 1):
             if batch < NBATCH:
-                anomaly, direct, cross, rows = solve_begin(batch)
+                anomaly, direct, rows = solve_begin(batch)
                 near(batch, anomaly)
-                values = flat(rows)
-            else:
-                values = ()
-
-            def step_body(step, values):
+            for step in range(8):
                 if batch > 0:
                     tile_step(batch - 1, f_ref if batch == 1 else o_ref, step)
                 if batch < NBATCH:
-                    values = flat(eliminate_eight(nested(values, 2)))
-                return values
-
-            values = lax.fori_loop(0, 8, step_body, values)
+                    rows = eliminate_eight(rows, step)
             if batch < NBATCH:
-                solved = jnp.concatenate([row[1] for row in nested(values, 2)], axis=0)
-                gain = direct - dot(cross, solved, HIGHEST)
+                left = jnp.concatenate([row[0] for row in rows], axis=0).T[64:]
+                right = jnp.concatenate([row[1] for row in rows], axis=0)
+                gain = direct - dot(left, right, HIGHEST)
                 if batch < NBATCH - 1:
                     high = (batch + 1) * OBS_B
                     state_ref[:, high:] = state_ref[:, high:] + dot(

time: 54.5 us -> 48.6 us (0.89)
  Pallas kernels: 54.4 us -> 48.5 us
    pallas_call x1, Pallas kernels: 20.5 us -> 14.6 us  [analyse(): pl.pallas_call(functools.partial(analysis_kernel, axes), out_shape=jax.Sh...]
where the time goes in v4:
time: 48.6 us; the launch traced here: 48.5 us
  Pallas kernels  48.5 us (100%)
    pallas_call x1, Pallas kernels, forecast_and_gather(): pl.pallas_call(functools.partial(forecast_kernel, n_x, n_y), out_shape=(j...  33.9 us
    pallas_call x1, Pallas kernels, analyse(): pl.pallas_call(functools.partial(analysis_kernel, axes), out_shape=jax.Sh...  14.6 us

profile of v4, /device:TPU:1, one launch (start us, length us, event | category | flops | bytes accessed | tf_op | source)
XLA Modules:
  0.0 48.5 jit_solution(1320406235946720742)
XLA Ops:
  0.0 33.9 %forecast_and_gather.1 = (f32[192,2048]{1,0:T(8,128)S(1)}, f32[256,128]{1,0:T(8,128)S(1)}, f32[72,512]{1,0:T(8,128)S(1)}, f32[512,8]{1,0:T(8,128)S(1)}, bf16[512...) custom-call(f32[8,24,2048]{2,1,0:T(8,128)} %ens_hbm.1, ...), custom_call_target="tpu_custom_call" | custom-call | tf_op jit(solution)/shard_map/forecast_and_gather/pallas_call | solution.py:598
  33.9 14.6 %analysis.1 = f32[192,2048]{1,0:T(8,128)} custom-call(f32[192,2048]{1,0:T(8,128)S(1)} %get-tuple-element.13.f_ref, f32[256,128]{1,0:T(8,128)S(1)} %get-tuple-element.14.p_ref, f32[72,512]{1,0:T(8,128)S(1)} %get-tuple-element.15.rows_ref, f32[512,8]{1,0:T(8,128)S(1)} %get-tuple-element.16.cols_ref, bf16[512,128]{1,0:T(8,128)(2,1)S(1)} %get-tuple-element.17.select_ref, ...), custom_call_target="tpu_custom_call" | custom-call | tf_op jit(solution)/shard_map/analysis/pallas_call | solution.py:273

commit v5 on v4

--- a/solution.py
+++ b/solution.py
@@ -332,7 +332,7 @@
     f_ref, p_ref, rows_ref, cols_ref, select_ref, across_ref, down_ref, most_ref,
     ens_ref, w_ref, cell_ref, batch_ref, ints_ref, floats_ref,
     west_ref, east_ref, south_ref, north_ref, first_ref, last_ref,
-    data_ref, spread_ref, point_ref, mix_ref, edge_ref, found_ref,
+    data_ref, chosen_ref, spread_ref, point_ref, mix_ref, edge_ref, found_ref,
     part_ref, got_y_ref, sum_ref, got_x_ref, total_ref, all_ref,
     loads, halo_send, halo_recv, send_1, recv_1, send_2, recv_2, send_3, recv_3,
 ):
@@ -341,8 +341,21 @@
     cells = rows_x * rows_y
     n_obs = batch_ref.shape[1]
 
-    def peer(axis, index, count, step):
-        return {axis: lax.rem(index + step, count)}
+    n_z, n_side = n_x // 2, 4
+    z, core, column, line = lax.div(gx, 2), lax.rem(gx, 2), lax.div(gy, n_side), lax.rem(gy, n_side)
+
+    def hops(offset):
+        return min(offset[0], n_z - offset[0]) + sum(min(d, n_side - d) for d in offset[2:]) + 0.1 * offset[1]
+
+    layer = [(0, c, x, y) for c in range(2) for x in range(n_y // n_side) for y in range(n_side)][1:]
+    layer = sorted(layer, key=hops, reverse=True)
+    stack = sorted([(d, 0, 0, 0) for d in range(1, n_z)], key=hops, reverse=True)
+
+    def place_of(offset):
+        return (
+            2 * lax.rem(z + offset[0], n_z) + lax.rem(core + offset[1], 2),
+            n_side * lax.rem(column + offset[2], n_y // n_side) + lax.rem(line + offset[3], n_side),
+        )
 
     small = [
         pltpu.make_async_copy(src, dst, loads.at[i])
@@ -365,41 +378,49 @@
     load_weights.start()
 
     barrier = pltpu.get_barrier_semaphore()
-    for step in range(1, n_x):
-        pl.semaphore_signal(barrier, inc=1, device_id=peer("gx", gx, n_x, step), device_id_type=MESH)
-    for step in range(1, n_y):
-        pl.semaphore_signal(barrier, inc=1, device_id=peer("gy", gy, n_y, step), device_id_type=MESH)
-
-    for copy in small:
-        copy.wait()
-    data_ref[0:3, :] = cell_ref[...].astype(F32)
-    data_ref[3:4, :] = ints_ref[...].astype(F32)
-    data_ref[4:5, :] = floats_ref[0]
-    data_ref[5:6, :] = floats_ref[1]
-    data_ref[6:8, :] = jnp.zeros((2, n_obs), F32)
-    data_ref[72:128, :] = jnp.zeros((56, n_obs), F32)
+    beside_x = lax.rem(gx + 2 * core - 1 + n_x, n_x)
+    for other in [(beside_x, gy)] + [place_of(offset) for offset in layer + stack]:
+        pl.semaphore_signal(barrier, inc=1, device_id=other, device_id_type=MESH)
+
     square = (n_obs, n_obs)
     at_row, at_lane = lax.broadcasted_iota(jnp.int32, square, 0), lax.broadcasted_iota(jnp.int32, square, 1)
     before = (at_row < at_lane).astype(F32).astype(BF16)
     kind = lax.broadcasted_iota(jnp.int32, (8, n_obs), 0)
+    for copy in small[:2]:
+        copy.wait()
     same = (kind == batch_ref[...]).astype(F32)
     count = dot(same.astype(BF16), before)
     rank = jnp.sum(same * (count + (kind * OBS_B).astype(F32)), axis=0, keepdims=True)
-    chosen = (at_row.astype(F32) == rank).astype(F32).astype(BF16)
-    data = data_ref[...]
-    high = data.astype(BF16)
-    middle, low = split(data - high.astype(F32))
-    thirds = dot_nt(chosen, jnp.concatenate([high, middle, low], axis=0))
-    table = (thirds[:, 0:128] + thirds[:, 128:256]) + thirds[:, 256:384]
-    cols_ref[...] = table[:, 0:8]
-    rows_ref[...] = table.T[0:72]
+    chosen_ref[...] = (at_row.astype(F32) == rank).astype(F32).astype(BF16)
+    cell = cell_ref[...].astype(F32)
+    half_y = jnp.floor(cell[1:2] * 0.5)
+    facts = jnp.where(kind == 2, cell[1:2] - 2.0 * half_y, jnp.where(kind == 3, cell[2:3], 0.0))
+    facts = jnp.where(kind == 0, cell[0:1], jnp.where(kind == 1, half_y, facts))
+    where = dot_nt(chosen_ref[...], facts.astype(BF16))
+
+    def order_all():
+        for copy in small[2:]:
+            copy.wait()
+        data_ref[0:3, :] = cell_ref[...].astype(F32)
+        data_ref[3:4, :] = ints_ref[...].astype(F32)
+        data_ref[4:5, :] = floats_ref[0]
+        data_ref[5:6, :] = floats_ref[1]
+        data_ref[6:8, :] = jnp.zeros((2, n_obs), F32)
+        data_ref[72:128, :] = jnp.zeros((56, n_obs), F32)
+        data = data_ref[...]
+        high = data.astype(BF16)
+        middle, low = split(data - high.astype(F32))
+        thirds = dot_nt(chosen_ref[...], jnp.concatenate([high, middle, low], axis=0))
+        table = (thirds[:, 0:128] + thirds[:, 128:256]) + thirds[:, 256:384]
+        cols_ref[...] = table[:, 0:8]
+        rows_ref[...] = table.T[0:72]
 
     load_tile.wait()
     for x in range(rows_x):
         first_ref[x : x + 1, :] = ens_ref[x, 0:1, :]
         last_ref[x : x + 1, :] = ens_ref[x, rows_y - 1 : rows_y, :]
 
-    pl.semaphore_wait(barrier, n_x + n_y - 2)
+    pl.semaphore_wait(barrier, len(layer) + len(stack) + 1)
 
     def halo(slot, src, dst, axis, target):
         return pltpu.make_async_remote_copy(
@@ -428,9 +449,9 @@
             merged = jnp.where(group == k, pltpu.roll(block, turn, 1) if turn else block, merged)
         point_ref[pl.ds(y, rows_x, stride=rows_y), :] = merged
 
-    obs_x = table[:, 0:1] - (gx * rows_x).astype(F32)
-    obs_y = table[:, 1:2] - (gy * rows_y).astype(F32)
-    obs_l = table[:, 2:3]
+    obs_x = where[:, 0:1] - (gx * rows_x).astype(F32)
+    obs_y = 2.0 * where[:, 1:2] + where[:, 2:3] - (gy * rows_y).astype(F32)
+    obs_l = where[:, 3:4]
     inside = (obs_x >= 0.0) & (obs_x < rows_x) & (obs_y >= 0.0) & (obs_y < rows_y)
 
     def place(value):
@@ -473,14 +494,14 @@
         found = found_ref[...]
         for h in range(2):
             found = jnp.where(
-                pair == (2 * step + h).astype(F32), found + here[:, h * 128 : h * 128 + 128], found
+                pair == 2.0 * step + h, found + here[:, h * 128 : h * 128 + 128], found
             )
         found_ref[...] = found
 
     def lanes_of(step):
-        return pl.ds(pl.multiple_of(step * 256, 256), 256)
-
-    def own_cells(step, carry):
+        return pl.ds(step * 256, 256)
+
+    def own_cells(step):
         high, low = split(ens_ref[:, :, lanes_of(step)].reshape(cells, 256))
         take(
             step,
@@ -488,9 +509,9 @@
             + dot(mix_ref[:, 256 : 256 + cells], high)
             + dot(mix_ref[:, 0:cells], low),
         )
-        return carry
-
-    lax.fori_loop(0, 8, own_cells, 0)
+
+    for step in range(8):
+        own_cells(step)
 
     for copy, _, receives, halo_ref in copies:
         pl.when(receives)(copy.wait_recv)
@@ -499,17 +520,17 @@
         def _():
             halo_ref[...] = jnp.zeros(halo_ref.shape, F32)
 
-    def cells_beside(step, carry):
+    def cells_beside(step):
         lanes = lanes_of(step)
         high, low = split(
             jnp.concatenate([west_ref[:, lanes], east_ref[:, lanes], south_ref[:, lanes], north_ref[:, lanes]], axis=0)
         )
         take(step, dot(edge_ref[...], jnp.concatenate([high, high, low], axis=0)))
-        return carry
-
-    lax.fori_loop(0, 8, cells_beside, 0)
-
-    def forecast_step(step, carry):
+
+    for step in range(8):
+        cells_beside(step)
+
+    def forecast_step(step):
         lanes = lanes_of(step)
         level = lax.broadcasted_iota(jnp.int32, (128, 256), 0)
         column = lax.broadcasted_iota(jnp.int32, (128, 256), 1) // 64 + 4 * step
@@ -528,7 +549,6 @@
                 at = k * cells + x * rows_y
                 total = total + weights[at : at + rows_y] * (other - q)
             f_ref[x * rows_y : x * rows_y + rows_y, lanes] = total
-        return carry
 
     found = found_ref[...]
     turned = pltpu.roll(found, 64, 1)
@@ -538,45 +558,46 @@
     side = lax.broadcasted_iota(jnp.int32, (half, 128), 1)
     part_ref[...] = jnp.where(side < 64, left[:half], right[half:])
 
-    share = half // n_y
-
-    def send(step, axis, index, count, src, dst, sends, recvs):
+    share = half // (len(layer) + 1)
+
+    def rows_of(place):
+        return pl.ds(pl.multiple_of((lax.rem(place[0], 2) * n_y + place[1]) * share, share), share)
+
+    def send(slot, offset, src, dst, sends, recvs):
         return pltpu.make_async_remote_copy(
-            src_ref=src, dst_ref=dst, send_sem=sends.at[step], recv_sem=recvs.at[step],
-            device_id=peer(axis, index, count, step), device_id_type=MESH,
-        )
-
-    def rows_of(index):
-        return pl.ds(pl.multiple_of(index * share, share), share)
+            src_ref=src, dst_ref=dst, send_sem=sends.at[slot], recv_sem=recvs.at[slot],
+            device_id=place_of(offset), device_id_type=MESH,
+        )
 
     first = [
-        send(s, "gy", gy, n_y, part_ref.at[rows_of(lax.rem(gy + s, n_y))], got_y_ref.at[s], send_1, recv_1)
-        for s in range(1, n_y)
+        send(s, offset, part_ref.at[rows_of(place_of(offset))], got_y_ref.at[s], send_1, recv_1)
+        for s, offset in enumerate(layer)
     ]
     for copy in first:
         copy.start()
+    order_all()
     tables(gx * rows_x, gy * rows_y, rows_ref, select_ref, across_ref, down_ref, most_ref)
-    lax.fori_loop(0, 2, forecast_step, 0)
-    total = part_ref[rows_of(gy), :]
-    for s, copy in enumerate(first, 1):
+    mine = rows_of((gx, gy))
+    total = part_ref[mine, :]
+    for s, copy in enumerate(first):
         copy.wait_recv()
         total = total + got_y_ref[s]
     sum_ref[...] = total
-    second = [send(s, "gx", gx, n_x, sum_ref, got_x_ref.at[s], send_2, recv_2) for s in range(1, n_x)]
+    second = [send(s, offset, sum_ref, got_x_ref.at[s], send_2, recv_2) for s, offset in enumerate(stack)]
     for copy in second:
         copy.start()
-    lax.fori_loop(2, 5, forecast_step, 0)
-    for s, copy in enumerate(second, 1):
+    for step in range(0, 5):
+        forecast_step(step)
+    for s, copy in enumerate(second):
         copy.wait_recv()
         total = total + got_x_ref[s]
     total_ref[...] = total
-    third = [
-        send(s, "gy", gy, n_y, total_ref, all_ref.at[rows_of(gy)], send_3, recv_3) for s in range(1, n_y)
-    ]
+    third = [send(s, offset, total_ref, all_ref.at[mine], send_3, recv_3) for s, offset in enumerate(layer)]
     for copy in third:
         copy.start()
-    all_ref[rows_of(gy), :] = total
-    lax.fori_loop(5, 8, forecast_step, 0)
+    all_ref[mine, :] = total
+    for step in range(5, 8):
+        forecast_step(step)
     for copy, sends, _, _ in copies:
         pl.when(sends)(copy.wait_send)
     for copy in first + second:
@@ -592,7 +613,8 @@
     rows_x, rows_y, width = ensemble.shape
     cells = rows_x * rows_y
     n_obs = obs_batch.shape[0]
-    share = n_obs // 2 // n_y
+    layer, stack = 2 * n_y, n_x // 2
+    share = n_obs // 2 // layer
     vmem = pl.BlockSpec(memory_space=pltpu.VMEM)
     dma = pltpu.SemaphoreType.DMA
     return pl.pallas_call(
@@ -623,19 +645,21 @@
             pltpu.VMEM((rows_x, width), F32),
             pltpu.VMEM((rows_x, width), F32),
             pltpu.VMEM((128, n_obs), F32),
+            pltpu.VMEM((n_obs, n_obs), BF16),
             pltpu.VMEM((4 * cells, 128), F32),
             pltpu.VMEM((cells, 128), F32),
             pltpu.VMEM((n_obs, 512), BF16),
             pltpu.VMEM((n_obs, 192), BF16),
             pltpu.VMEM((n_obs, 128), F32),
             pltpu.VMEM((n_obs // 2, 128), F32),
-            pltpu.VMEM((n_y, share, 128), F32),
+            pltpu.VMEM((layer - 1, share, 128), F32),
             pltpu.VMEM((share, 128), F32),
-            pltpu.VMEM((n_x, share, 128), F32),
+            pltpu.VMEM((stack - 1, share, 128), F32),
             pltpu.VMEM((share, 128), F32),
             pltpu.VMEM((n_obs // 2, 128), F32),
             dma((8,)), dma((4,)), dma((4,)),
-            dma((n_y,)), dma((n_y,)), dma((n_x,)), dma((n_x,)), dma((n_y,)), dma((n_y,)),
+            dma((layer - 1,)), dma((layer - 1,)), dma((stack - 1,)), dma((stack - 1,)),
+            dma((layer - 1,)), dma((layer - 1,)),
         ],
         compiler_params=pltpu.CompilerParams(
             collective_id=0, has_side_effects=True, vmem_limit_bytes=48 * 1024 * 1024

time: 48.6 us -> 46 us (0.947)
  Pallas kernels: 48.5 us -> 45.9 us
    pallas_call x1, Pallas kernels: 33.9 us -> 31.3 us  [forecast_and_gather(): pl.pallas_call(functools.partial(forecast_kernel, n_x, n_y), out_shape=(j...]
where the time goes in v5:
time: 46 us; the launch traced here: 45.9 us
  Pallas kernels  45.9 us (100%)
    pallas_call x1, Pallas kernels, forecast_and_gather(): pl.pallas_call(functools.partial(forecast_kernel, n_x, n_y), out_shape=(j...  31.3 us
    pallas_call x1, Pallas kernels, analyse(): pl.pallas_call(functools.partial(analysis_kernel, axes), out_shape=jax.Sh...  14.6 us

profile of v5, /device:TPU:1, one launch (start us, length us, event | category | flops | bytes accessed | tf_op | source)
XLA Modules:
  0.0 45.9 jit_solution(13553511094790665739)
XLA Ops:
  0.0 31.3 %forecast_and_gather.1 = (f32[192,2048]{1,0:T(8,128)S(1)}, f32[256,128]{1,0:T(8,128)S(1)}, f32[72,512]{1,0:T(8,128)S(1)}, f32[512,8]{1,0:T(8,128)S(1)}, bf16[512...) custom-call(f32[8,24,2048]{2,1,0:T(8,128)} %ens_hbm.1, ...), custom_call_target="tpu_custom_call" | custom-call | tf_op jit(solution)/shard_map/forecast_and_gather/pallas_call | solution.py:620
  31.3 14.6 %analysis.1 = f32[192,2048]{1,0:T(8,128)} custom-call(f32[192,2048]{1,0:T(8,128)S(1)} %get-tuple-element.13.f_ref, f32[256,128]{1,0:T(8,128)S(1)} %get-tuple-element.14.p_ref, f32[72,512]{1,0:T(8,128)S(1)} %get-tuple-element.15.rows_ref, f32[512,8]{1,0:T(8,128)S(1)} %get-tuple-element.16.cols_ref, bf16[512,128]{1,0:T(8,128)(2,1)S(1)} %get-tuple-element.17.select_ref, ...), custom_call_target="tpu_custom_call" | custom-call | tf_op jit(solution)/shard_map/analysis/pallas_call | solution.py:273

commit v6 on v5

--- a/solution.py
+++ b/solution.py
@@ -67,7 +67,7 @@
     shape = (8, 128)
     four = range(4)
     columns = [
-        [jnp.broadcast_to(rows[v][0][:, low + j : low + j + 1], shape) for v in range(block, len(rows))]
+        [jnp.take_along_axis(rows[v][0], jnp.full(shape, low + j, jnp.int32), axis=1, mode='promise_in_bounds') for v in range(block, len(rows))]
         for j in range(8)
     ]
 

time: 46 us -> 44.3 us (0.963)
  Pallas kernels: 45.9 us -> 44.2 us
    pallas_call x1, Pallas kernels: 14.6 us -> 13 us  [analyse(): pl.pallas_call(functools.partial(analysis_kernel, axes), out_shape=jax.Sh...]
where the time goes in v6:
time: 44.3 us; the launch traced here: 44.2 us
  Pallas kernels  44.2 us (100%)
    pallas_call x1, Pallas kernels, forecast_and_gather(): pl.pallas_call(functools.partial(forecast_kernel, n_x, n_y), out_shape=(j...  31.3 us
    pallas_call x1, Pallas kernels, analyse(): pl.pallas_call(functools.partial(analysis_kernel, axes), out_shape=jax.Sh...  13 us

profile of v6, /device:TPU:1, one launch (start us, length us, event | category | flops | bytes accessed | tf_op | source)
XLA Modules:
  0.0 44.2 jit_solution(14153054333331883486)
XLA Ops:
  0.0 31.3 %forecast_and_gather.1 = (f32[192,2048]{1,0:T(8,128)S(1)}, f32[256,128]{1,0:T(8,128)S(1)}, f32[72,512]{1,0:T(8,128)S(1)}, f32[512,8]{1,0:T(8,128)S(1)}, bf16[512...) custom-call(f32[8,24,2048]{2,1,0:T(8,128)} %ens_hbm.1, ...), custom_call_target="tpu_custom_call" | custom-call | tf_op jit(solution)/shard_map/forecast_and_gather/pallas_call | solution.py:620
  31.3 13.0 %analysis.1 = f32[192,2048]{1,0:T(8,128)} custom-call(f32[192,2048]{1,0:T(8,128)S(1)} %get-tuple-element.13.f_ref, f32[256,128]{1,0:T(8,128)S(1)} %get-tuple-element.14.p_ref, f32[72,512]{1,0:T(8,128)S(1)} %get-tuple-element.15.rows_ref, f32[512,8]{1,0:T(8,128)S(1)} %get-tuple-element.16.cols_ref, bf16[512,128]{1,0:T(8,128)(2,1)S(1)} %get-tuple-element.17.select_ref, ...), custom_call_target="tpu_custom_call" | custom-call | tf_op jit(solution)/shard_map/analysis/pallas_call | solution.py:273

commit v7 on v6

--- a/solution.py
+++ b/solution.py
@@ -71,8 +71,12 @@
         for j in range(8)
     ]
 
+    pivots = [jnp.broadcast_to(rows[block][0][i : i + 1, :], shape) for i in range(8)]
+
     def entry(i, j):
-        return jnp.broadcast_to(columns[j][0][i : i + 1, :], shape)
+        return jnp.take_along_axis(
+            pivots[i], jnp.full(shape, low + j, jnp.int32), axis=1, mode='promise_in_bounds'
+        )
 
     first = [[entry(i, j) for j in range(i + 1)] for i in four]
     cross = [[entry(4 + i, j) for j in four] for i in four]

time: 44.3 us -> 44.6 us (level)
  no operation moved by 1% of the time
where the time goes in v7:
time: 44.6 us; the launch traced here: 44.5 us
  Pallas kernels  44.4 us (100%)
    pallas_call x1, Pallas kernels, forecast_and_gather(): pl.pallas_call(functools.partial(forecast_kernel, n_x, n_y), out_shape=(j...  31.3 us
    pallas_call x1, Pallas kernels, analyse(): pl.pallas_call(functools.partial(analysis_kernel, axes), out_shape=jax.Sh...  13.2 us

profile of v7, /device:TPU:1, one launch (start us, length us, event | category | flops | bytes accessed | tf_op | source)
XLA Modules:
  0.0 44.5 jit_solution(2878418164918356043)
XLA Ops:
  0.0 31.3 %forecast_and_gather.1 = (f32[192,2048]{1,0:T(8,128)S(1)}, f32[256,128]{1,0:T(8,128)S(1)}, f32[72,512]{1,0:T(8,128)S(1)}, f32[512,8]{1,0:T(8,128)S(1)}, bf16[512...) custom-call(f32[8,24,2048]{2,1,0:T(8,128)} %ens_hbm.1, ...), custom_call_target="tpu_custom_call" | custom-call | tf_op jit(solution)/shard_map/forecast_and_gather/pallas_call | solution.py:624
  31.3 13.2 %analysis.1 = f32[192,2048]{1,0:T(8,128)} custom-call(f32[192,2048]{1,0:T(8,128)S(1)} %get-tuple-element.13.f_ref, f32[256,128]{1,0:T(8,128)S(1)} %get-tuple-element.14.p_ref, f32[72,512]{1,0:T(8,128)S(1)} %get-tuple-element.15.rows_ref, f32[512,8]{1,0:T(8,128)S(1)} %get-tuple-element.16.cols_ref, bf16[512,128]{1,0:T(8,128)(2,1)S(1)} %get-tuple-element.17.select_ref, ...), custom_call_target="tpu_custom_call" | custom-call | tf_op jit(solution)/shard_map/analysis/pallas_call | solution.py:277
